TPU v7x, 32 devices: a whole 2x2x4 slice. The times are simulated.
32 devices in a mesh: ctx: 8 (over z, y), fsdp: 4 (over x, core).
Axes of the slice: x: 2, y: 2, z: 4, core: 2. Of those that a mesh axis runs over, the one named last changes fastest.
Arguments:
- inputs: bfloat16 [16, 8, 2, 64, 960], P('fsdp', 'ctx'), may hold values from -6 to 6
- attn_gain: bfloat16 [960], P('fsdp'), may hold values from 0.099609375 to 1.8984375
- query_weight: bfloat16 [960, 960], P('fsdp'), may hold values from -0.1875 to 0.1875
- key_projection_weight: bfloat16 [960, 320], P('fsdp'), may hold values from -0.1875 to 0.1875
- value_projection_weight: bfloat16 [960, 320], P('fsdp'), may hold values from -0.1875 to 0.1875
- out_weight: bfloat16 [960, 960], P('fsdp'), may hold values from -1.5 to 1.5
- ffn_gain: bfloat16 [960], P('fsdp'), may hold values from 0.099609375 to 1.8984375
- gate_weight: bfloat16 [960, 2560], P('fsdp'), may hold values from -0.1875 to 0.1875
- up_weight: bfloat16 [960, 2560], P('fsdp'), may hold values from -0.1875 to 0.1875
- down_weight: bfloat16 [2560, 960], P('fsdp'), may hold values from -0.125 to 0.125
- positions: int32 [16, 8, 2, 64], P('fsdp', 'ctx'), may hold values from 0 to 2046, as said below
- cotangent: bfloat16 [16, 8, 2, 64, 960], P('fsdp', 'ctx'), may hold values from -6 to 6
Outputs:
- outputs: bfloat16 [16, 8, 2, 64, 960], P('fsdp', 'ctx')
- input_grad: float32 [16, 8, 2, 64, 960], P('fsdp', 'ctx')
- attn_gain_grad: float32 [960], P('fsdp')
- query_grad: float32 [960, 960], P('fsdp', 'ctx')
- key_grad: float32 [960, 320], P('fsdp', 'ctx')
- value_grad: float32 [960, 320], P('fsdp', 'ctx')
- out_grad: float32 [960, 960], P('fsdp', 'ctx')
- ffn_gain_grad: float32 [960], P('fsdp')
- gate_grad: float32 [960, 2560], P('fsdp', 'ctx')
- up_grad: float32 [960, 2560], P('fsdp', 'ctx')
- down_grad: float32 [2560, 960], P('fsdp', 'ctx')
Inputs may be any that keep to these rules, and one draw needn't show every extreme that they name: `positions`: within each sequence, in token order, the first position is 0 and each next one is larger by 1 or 2.
All inputs are finite; a program needn't handle non-finite values.
Results may differ from a plain program's by a relative error of at most 0.019.
Values may be sent and summed in bfloat16 or wider, within the bound.
No kernel may reach another device: no remote copies, remote signals or barrier semaphores. Data moves between devices by JAX's collectives and lax.ppermute only.
A program may use at most 256 MiB of HBM per device.

v0:
```python
import jax
import jax.numpy as jnp
from jax import lax
from jax.sharding import PartitionSpec as P

QUERY_HEADS = 15
KEY_VALUE_HEADS = 5
HEAD_SIZE = 64


eps = 1e-05
theta_base = 100000.0


def rope_tables(positions):
    half = HEAD_SIZE // 2
    freqs = theta_base ** (-jnp.arange(half, dtype=jnp.float32) * 2.0 / HEAD_SIZE)
    freqs = jnp.concatenate([freqs, freqs])
    angles = positions.astype(jnp.float32)[..., None, None] * freqs
    return (jnp.cos(angles), jnp.sin(angles))


def rotate(value_rows):
    half = value_rows.shape[-1] // 2
    return jnp.concatenate([-value_rows[..., half:], value_rows[..., :half]], axis=-1)


def rotate_pairs(value_rows, cosine_table, sine_table):
    return value_rows * cosine_table + rotate(value_rows) * sine_table


def rotate_pairs_back(grads, cosine_table, sine_table):
    return grads * cosine_table - rotate(grads * sine_table)


def norm_forward(value_rows, gain):
    inverse = lax.rsqrt(jnp.mean(value_rows * value_rows, axis=-1, keepdims=True) + eps)
    return (value_rows * inverse * gain, inverse)


def norm_backward(value_rows, inverse, gain, grad_normed):
    scaled = grad_normed * gain
    gain_grad = jnp.sum(grad_normed * value_rows * inverse, axis=0)
    value_grad = inverse * scaled - value_rows * inverse**3 * jnp.mean(
        scaled * value_rows, axis=-1, keepdims=True
    )
    return (value_grad, gain_grad)


def score_block(query_part, key_part, query_index, key_index, scale):
    scores = (
        jnp.einsum("gqd,kd->gqk", query_part, key_part, preferred_element_type=jnp.float32) * scale
    )
    allowed = key_index[None, :] <= query_index[:, None]
    return jnp.where(allowed[None], scores, -1e30)


def attend(query_part, key_part, value_part, query_index, key_index, scale):
    scores = score_block(query_part, key_part, query_index, key_index, scale)
    top = jnp.max(scores, axis=-1, keepdims=True)
    weights = jnp.exp(scores - top)
    total = jnp.sum(weights, axis=-1, keepdims=True)
    probs = (weights / total).astype(jnp.bfloat16)
    mixed = jnp.einsum("gqk,kd->gqd", probs, value_part, preferred_element_type=jnp.float32)
    return (mixed, (top + jnp.log(total))[..., 0])


def attend_back(
    query_part, key_part, value_part, log_total, grad_mixed, query_index, key_index, scale
):
    scores = score_block(query_part, key_part, query_index, key_index, scale)
    probs = jnp.exp(scores - log_total[..., None])
    probs_low = probs.astype(jnp.bfloat16)
    grad_probs = jnp.einsum(
        "gqd,kd->gqk", grad_mixed, value_part, preferred_element_type=jnp.float32
    )
    inner = jnp.sum(probs * grad_probs, axis=-1, keepdims=True)
    grad_scores = (probs * (grad_probs - inner)).astype(jnp.bfloat16)
    grad_query = (
        jnp.einsum("gqk,kd->gqd", grad_scores, key_part, preferred_element_type=jnp.float32) * scale
    )
    grad_keys = (
        jnp.einsum("gqk,gqd->kd", grad_scores, query_part, preferred_element_type=jnp.float32)
        * scale
    )
    grad_values = jnp.einsum(
        "gqk,gqd->kd", probs_low, grad_mixed, preferred_element_type=jnp.float32
    )
    return (grad_query, grad_keys, grad_values)


def shards(
    inputs,
    attn_gain,
    query_weight,
    key_projection_weight,
    value_projection_weight,
    out_weight,
    ffn_gain,
    gate_weight,
    up_weight,
    down_weight,
    positions,
    cotangent,
):
    sequence_batch = inputs.shape[0]
    block = inputs.shape[3]
    width = inputs.shape[4]
    pairs = lax.axis_size("ctx")
    token_rows = sequence_batch * 2 * block
    head_group = QUERY_HEADS // KEY_VALUE_HEADS
    query_token_rows = 2 * block
    key_rows_total = pairs * 2 * block
    key_value_width = KEY_VALUE_HEADS * HEAD_SIZE
    scale = HEAD_SIZE ** (-0.5)
    first_gain, query_full, key_full, value_full, out_full = (
        lax.all_gather(attn_gain, "fsdp", axis=0, tiled=True),
        lax.all_gather(query_weight, "fsdp", axis=0, tiled=True),
        lax.all_gather(key_projection_weight, "fsdp", axis=0, tiled=True),
        lax.all_gather(value_projection_weight, "fsdp", axis=0, tiled=True),
        lax.all_gather(out_weight, "fsdp", axis=0, tiled=True),
    )
    first_gain = first_gain.astype(jnp.float32)
    residual_in = inputs.reshape(token_rows, width).astype(jnp.float32)
    cosine_table, sine_table = rope_tables(positions.reshape(token_rows))
    normalized_input, inverse_first = norm_forward(residual_in, first_gain)
    normed_low = normalized_input.astype(jnp.bfloat16)
    query_proj = jnp.dot(normed_low, query_full, preferred_element_type=jnp.float32)
    key_projected = jnp.dot(normed_low, key_full, preferred_element_type=jnp.float32)
    value_proj = jnp.dot(normed_low, value_full, preferred_element_type=jnp.float32)
    query_low = rotate_pairs(
        query_proj.reshape(token_rows, QUERY_HEADS, HEAD_SIZE), cosine_table, sine_table
    ).astype(jnp.bfloat16)
    key_reduced = rotate_pairs(
        key_projected.reshape(token_rows, KEY_VALUE_HEADS, HEAD_SIZE), cosine_table, sine_table
    ).astype(jnp.bfloat16)
    key_reduced = key_reduced.reshape(sequence_batch, 1, 2, block, key_value_width)
    value_low = value_proj.astype(jnp.bfloat16).reshape(
        sequence_batch, 1, 2, block, key_value_width
    )
    key_all, value_all = (
        lax.all_gather(key_reduced, "ctx", axis=1, tiled=True),
        lax.all_gather(value_low, "ctx", axis=1, tiled=True),
    )
    ctx_index = lax.axis_index("ctx")
    own_blocks = jnp.stack([ctx_index, 2 * pairs - 1 - ctx_index])
    query_index = (own_blocks[:, None] * block + jnp.arange(block)[None, :]).reshape(
        query_token_rows
    )
    block_ids = jnp.arange(pairs)
    every_block = jnp.stack([block_ids, 2 * pairs - 1 - block_ids], axis=1)
    key_index = (every_block[:, :, None] * block + jnp.arange(block)[None, None, :]).reshape(
        key_rows_total
    )

    def by_head(value_rows):
        return (
            value_rows.reshape(sequence_batch, key_rows_total, KEY_VALUE_HEADS, HEAD_SIZE)
            .transpose(0, 2, 1, 3)
            .reshape(sequence_batch * KEY_VALUE_HEADS, key_rows_total, HEAD_SIZE)
        )

    def to_items(value_rows):
        return (
            value_rows.reshape(
                sequence_batch, query_token_rows, KEY_VALUE_HEADS, head_group, HEAD_SIZE
            )
            .transpose(0, 2, 3, 1, 4)
            .reshape(sequence_batch * KEY_VALUE_HEADS, head_group, query_token_rows, HEAD_SIZE)
        )

    def from_items(value_rows):
        return (
            value_rows.reshape(
                sequence_batch, KEY_VALUE_HEADS, head_group, query_token_rows, HEAD_SIZE
            )
            .transpose(0, 3, 1, 2, 4)
            .reshape(token_rows, QUERY_HEADS, HEAD_SIZE)
        )

    def unhead(value_rows):
        return (
            value_rows.reshape(sequence_batch, KEY_VALUE_HEADS, key_rows_total, HEAD_SIZE)
            .transpose(0, 2, 1, 3)
            .reshape(sequence_batch, pairs, 2, block, key_value_width)
        )

    query_items = to_items(query_low)
    key_items = by_head(key_all)
    value_items = by_head(value_all)

    def forward_item(item):
        return attend(item[0], item[1], item[2], query_index, key_index, scale)

    mixed_items, total_items = lax.map(forward_item, (query_items, key_items, value_items))
    mixed_low = (
        from_items(mixed_items).reshape(token_rows, QUERY_HEADS * HEAD_SIZE).astype(jnp.bfloat16)
    )
    branch = jnp.dot(mixed_low, out_full, preferred_element_type=jnp.float32)
    hidden = residual_in + branch
    second_gain, gate_full, up_full, down_full = (
        lax.all_gather(ffn_gain, "fsdp", axis=0, tiled=True),
        lax.all_gather(gate_weight, "fsdp", axis=0, tiled=True),
        lax.all_gather(up_weight, "fsdp", axis=0, tiled=True),
        lax.all_gather(down_weight, "fsdp", axis=0, tiled=True),
    )
    second_gain = second_gain.astype(jnp.float32)
    normed_ffn, inverse_second = norm_forward(hidden, second_gain)
    normed_ffn_low = normed_ffn.astype(jnp.bfloat16)
    gate = jnp.dot(normed_ffn_low, gate_full, preferred_element_type=jnp.float32)
    up_part = jnp.dot(normed_ffn_low, up_full, preferred_element_type=jnp.float32)
    sigmoid_gate = jax.nn.sigmoid(gate)
    act_low = (gate * sigmoid_gate * up_part).astype(jnp.bfloat16)
    ffn_out = jnp.dot(act_low, down_full, preferred_element_type=jnp.float32)
    outputs = (hidden + ffn_out).astype(jnp.bfloat16).reshape(inputs.shape)
    grad_low = cotangent.reshape(token_rows, width)
    down_grad = jnp.einsum("rf,rd->fd", act_low, grad_low, preferred_element_type=jnp.float32)
    grad_act = jnp.einsum("rd,fd->rf", grad_low, down_full, preferred_element_type=jnp.float32)
    grad_up = (grad_act * gate * sigmoid_gate).astype(jnp.bfloat16)
    grad_gate = (grad_act * up_part * sigmoid_gate * (1.0 + gate * (1.0 - sigmoid_gate))).astype(
        jnp.bfloat16
    )
    gate_grad = jnp.einsum(
        "rd,rf->df", normed_ffn_low, grad_gate, preferred_element_type=jnp.float32
    )
    up_grad = jnp.einsum("rd,rf->df", normed_ffn_low, grad_up, preferred_element_type=jnp.float32)
    grad_normed_ffn = jnp.einsum(
        "rf,df->rd", grad_gate, gate_full, preferred_element_type=jnp.float32
    )
    grad_normed_ffn = grad_normed_ffn + jnp.einsum(
        "rf,df->rd", grad_up, up_full, preferred_element_type=jnp.float32
    )
    grad_through, ffn_gain_grad = norm_backward(
        hidden, inverse_second, second_gain, grad_normed_ffn
    )
    grad_hidden = grad_low.astype(jnp.float32) + grad_through
    grad_branch = grad_hidden.astype(jnp.bfloat16)
    out_grad = jnp.einsum("re,rd->ed", mixed_low, grad_branch, preferred_element_type=jnp.float32)
    grad_mixed = jnp.einsum(
        "rd,ed->re", grad_branch, out_full, preferred_element_type=jnp.float32
    ).astype(jnp.bfloat16)
    grad_items = to_items(grad_mixed)

    def backward_item(item):
        return attend_back(
            item[0], item[1], item[2], item[3], item[4], query_index, key_index, scale
        )

    query_back, key_back, value_back = lax.map(
        backward_item, (query_items, key_items, value_items, total_items, grad_items)
    )
    key_gradient_sum, value_sum = (
        lax.psum_scatter(unhead(key_back), "ctx", scatter_dimension=1, tiled=True),
        lax.psum_scatter(unhead(value_back), "ctx", scatter_dimension=1, tiled=True),
    )
    grad_query_low = (
        rotate_pairs_back(from_items(query_back), cosine_table, sine_table)
        .reshape(token_rows, QUERY_HEADS * HEAD_SIZE)
        .astype(jnp.bfloat16)
    )
    grad_key_low = (
        rotate_pairs_back(
            key_gradient_sum.reshape(token_rows, KEY_VALUE_HEADS, HEAD_SIZE),
            cosine_table,
            sine_table,
        )
        .reshape(token_rows, key_value_width)
        .astype(jnp.bfloat16)
    )
    grad_value_low = value_sum.reshape(token_rows, key_value_width).astype(jnp.bfloat16)
    query_grad = jnp.einsum(
        "rd,re->de", normed_low, grad_query_low, preferred_element_type=jnp.float32
    )
    key_grad = jnp.einsum("rd,re->de", normed_low, grad_key_low, preferred_element_type=jnp.float32)
    value_grad = jnp.einsum(
        "rd,re->de", normed_low, grad_value_low, preferred_element_type=jnp.float32
    )
    grad_normed = jnp.einsum(
        "re,de->rd", grad_query_low, query_full, preferred_element_type=jnp.float32
    )
    grad_normed = grad_normed + jnp.einsum(
        "re,de->rd", grad_key_low, key_full, preferred_element_type=jnp.float32
    )
    grad_normed = grad_normed + jnp.einsum(
        "re,de->rd", grad_value_low, value_full, preferred_element_type=jnp.float32
    )
    grad_input, attn_gain_grad = norm_backward(residual_in, inverse_first, first_gain, grad_normed)
    input_grad = (grad_hidden + grad_input).reshape(inputs.shape)
    (
        attn_gain_grad,
        ffn_gain_grad,
        query_grad,
        key_grad,
        value_grad,
        out_grad,
        gate_grad,
        up_grad,
        down_grad,
    ) = (
        lax.psum_scatter(
            attn_gain_grad.astype(jnp.bfloat16), "fsdp", scatter_dimension=0, tiled=True
        ).astype(jnp.float32),
        lax.psum_scatter(
            ffn_gain_grad.astype(jnp.bfloat16), "fsdp", scatter_dimension=0, tiled=True
        ).astype(jnp.float32),
        lax.psum_scatter(
            query_grad.astype(jnp.bfloat16), "fsdp", scatter_dimension=0, tiled=True
        ).astype(jnp.float32),
        lax.psum_scatter(
            key_grad.astype(jnp.bfloat16), "fsdp", scatter_dimension=0, tiled=True
        ).astype(jnp.float32),
        lax.psum_scatter(
            value_grad.astype(jnp.bfloat16), "fsdp", scatter_dimension=0, tiled=True
        ).astype(jnp.float32),
        lax.psum_scatter(
            out_grad.astype(jnp.bfloat16), "fsdp", scatter_dimension=0, tiled=True
        ).astype(jnp.float32),
        lax.psum_scatter(
            gate_grad.astype(jnp.bfloat16), "fsdp", scatter_dimension=0, tiled=True
        ).astype(jnp.float32),
        lax.psum_scatter(
            up_grad.astype(jnp.bfloat16), "fsdp", scatter_dimension=0, tiled=True
        ).astype(jnp.float32),
        lax.psum_scatter(
            down_grad.astype(jnp.bfloat16), "fsdp", scatter_dimension=0, tiled=True
        ).astype(jnp.float32),
    )
    query_grad, key_grad, value_grad, out_grad, gate_grad, up_grad, down_grad = (
        lax.psum_scatter(
            query_grad.astype(jnp.bfloat16), "ctx", scatter_dimension=1, tiled=True
        ).astype(jnp.float32),
        lax.psum_scatter(
            key_grad.astype(jnp.bfloat16), "ctx", scatter_dimension=1, tiled=True
        ).astype(jnp.float32),
        lax.psum_scatter(
            value_grad.astype(jnp.bfloat16), "ctx", scatter_dimension=1, tiled=True
        ).astype(jnp.float32),
        lax.psum_scatter(
            out_grad.astype(jnp.bfloat16), "ctx", scatter_dimension=1, tiled=True
        ).astype(jnp.float32),
        lax.psum_scatter(
            gate_grad.astype(jnp.bfloat16), "ctx", scatter_dimension=1, tiled=True
        ).astype(jnp.float32),
        lax.psum_scatter(
            up_grad.astype(jnp.bfloat16), "ctx", scatter_dimension=1, tiled=True
        ).astype(jnp.float32),
        lax.psum_scatter(
            down_grad.astype(jnp.bfloat16), "ctx", scatter_dimension=1, tiled=True
        ).astype(jnp.float32),
    )
    attn_gain_grad, ffn_gain_grad = lax.psum((attn_gain_grad, ffn_gain_grad), "ctx")
    return (
        outputs,
        input_grad,
        attn_gain_grad,
        query_grad,
        key_grad,
        value_grad,
        out_grad,
        ffn_gain_grad,
        gate_grad,
        up_grad,
        down_grad,
    )


def solution(mesh):
    in_specs = (
        P("fsdp", "ctx", None, None, None),
        P("fsdp"),
        P("fsdp", None),
        P("fsdp", None),
        P("fsdp", None),
        P("fsdp", None),
        P("fsdp"),
        P("fsdp", None),
        P("fsdp", None),
        P("fsdp", None),
        P("fsdp", "ctx", None, None),
        P("fsdp", "ctx", None, None, None),
    )
    out_specs = (
        P("fsdp", "ctx", None, None, None),
        P("fsdp", "ctx", None, None, None),
        P("fsdp"),
        P("fsdp", "ctx"),
        P("fsdp", "ctx"),
        P("fsdp", "ctx"),
        P("fsdp", "ctx"),
        P("fsdp"),
        P("fsdp", "ctx"),
        P("fsdp", "ctx"),
        P("fsdp", "ctx"),
    )
    return jax.shard_map(shards, mesh=mesh, in_specs=in_specs, out_specs=out_specs, check_vma=False)
```

profile of v0, /device:TPU:0, one launch (start us, length us, event | category | flops | bytes accessed | tf_op | source)
XLA Modules:
  0.0 1540.6 jit_solution(12851870523670877826)
XLA Ops:
  11.7 8.3 all-reduce.7
  20.8 11.6 all-gather
  38.5 8.0 all-gather.1
  57.1 3.9 copy.162
  68.3 32.1 %all-gather.12.cloned.1.call-done = bf16[4,8,2,64,320]{4,3,2,0,1:T(8,128)(2,1)} async-done(((bf16[4,1,2,64,320]{4,3,2,0,1:T(8,128)(2,1)}), bf16[4,8,2,64,320]{4,3,2,0,1:T(8,128)(2,1)}) %all-gather.12.cloned.1.call-update) | async-done | bytes 2621456 | tf_op jit(solution)/shard_map/all_gather | solution.py:142
  100.4 11.6 copy.168
  111.9 12.2 reshape.452
  124.1 37.5 %all-gather.14.cloned.1.call-done = bf16[4,8,2,64,320]{4,3,2,0,1:T(8,128)(2,1)} async-done(((bf16[4,1,2,64,320]{4,3,2,0,1:T(8,128)(2,1)}), bf16[4,8,2,64,320]{4,3,2,0,1:T(8,128)(2,1)}) %all-gather.14.cloned.1.call-update) | async-done | bytes 2621456 | tf_op jit(solution)/shard_map/all_gather | solution.py:143
  161.7 11.6 copy.172
  173.3 12.3 reshape.455
  185.6 86.4 %while.30 = (s32[]{:T(128)}, bf16[20,3,128,64]{2,3,1,0:T(8,128)(2,1)S(1)}, f32[20,3,128]{2,1,0:T(4,128)}, bf16[20,3,128,64]{2,3,1,0:T(8,128)(2,1)}, bf16[20,1024...) while((s32[]{:T(128)}, ...), condition=%wide.region_4.5_spmd.clone.clone, body=%wide.region_1.4_spmd.clone.sunk.clone | while | flops 103940864 | bytes 5424809 | solution.py:195
  273.8 3.8 multiply_reduce_fusion.6
  279.1 7.4 fusion.70
  286.5 7.1 fusion.71
  293.7 10.3 all-gather.22.cloned.1.call-done
  303.9 10.0 multiply_convert_fusion.1
  314.0 6.6 fusion.72
  320.6 3.6 multiply_reduce_fusion.2
  331.4 222.8 %while.31 = (s32[]{:T(128)}, f32[20,3,128,64]{2,3,1,0:T(8,128)}, f32[20,1024,64]{1,2,0:T(8,128)}, f32[20,1024,64]{1,2,0:T(8,128)}, bf16[20,3,128,64]{2,3,1,0:T(8...) while((s32[]{:T(128)}, f32[20,3,128,64]{2,3,1,0:T(8,128)}, ...), condition=%wide.region_9.10_spmd.clone.clone, body=%wide.region_7.9_spmd.clone.sunk.clone | while | flops 255419136 | bytes 13302977 | solution.py:249
  554.2 11.8 reshape.465
  566.0 13.5 copy.181
  579.6 12.2 reshape.469
  591.8 13.6 copy.185
  605.5 4.2 copy.228
  621.0 4.5 convolution_convert_fusion.3
  625.5 72.2 %reduce-scatter.33.cloned.1.call-done = f32[4,1,2,64,320]{4,3,2,0,1:T(8,128)} async-done(((f32[4,8,2,64,320]{4,3,2,0,1:T(8,128)}), f32[4,1,2,64,320]{4,3,2,0,1:T(8,128)}) %reduce-scatter.33.cloned.1.call-update) | async-done | bytes 655376 | tf_op jit(solution)/shard_map/reduce_scatter | solution.py:253
  700.1 3.4 reshape.467
  709.7 108.8 %reduce-scatter.35.cloned.1.call-done = f32[4,1,2,64,320]{4,3,2,0,1:T(8,128)} async-done(((f32[4,8,2,64,320]{4,3,2,0,1:T(8,128)}), f32[4,1,2,64,320]{4,3,2,0,1:T(8,128)}) %reduce-scatter.35.cloned.1.call-update) | async-done | bytes 655376 | tf_op jit(solution)/shard_map/reduce_scatter | solution.py:254
  824.7 6.3 convolution_convert_fusion.2
  831.1 6.3 convolution_convert_fusion.1
  838.5 6.7 convolution_convert_fusion
  845.2 7.9 copy.211
  855.3 28.8 %reduce-scatter.43.cloned.1.call-done = bf16[240,960]{1,0:T(8,128)(2,1)} async-done(((bf16[960,960]{1,0:T(8,128)(2,1)}), bf16[240,960]{1,0:T(8,128)(2,1)}) %reduce-scatter.43.cloned.1.call-update) | async-done | bytes 460816 | tf_op jit(solution)/shard_map/reduce_scatter | solution.py:315
  886.2 23.3 %reduce-scatter.51.cloned.1.call-done = bf16[240,320]{1,0:T(8,128)(2,1)} async-done(((bf16[960,320]{1,0:T(8,128)(2,1)}), bf16[240,320]{1,0:T(8,128)(2,1)}) %reduce-scatter.51.cloned.1.call-update) | async-done | bytes 153616
  911.3 24.5 %reduce-scatter.53.cloned.1.call-done = bf16[240,320]{1,0:T(8,128)(2,1)} async-done(((bf16[960,320]{1,0:T(8,128)(2,1)}), bf16[240,320]{1,0:T(8,128)(2,1)}) %reduce-scatter.53.cloned.1.call-update) | async-done | bytes 153616
  937.6 49.9 %reduce-scatter.45.cloned.1.call-done = bf16[240,2560]{1,0:T(8,128)(2,1)} async-done(((bf16[960,2560]{1,0:T(8,128)(2,1)}), bf16[240,2560]{1,0:T(8,128)(2,1)}) %reduce-scatter.45.cloned.1.call-update) | async-done | bytes 1228816 | tf_op jit(solution)/shard_map/reduce_scatter | solution.py:318
  990.0 49.4 %reduce-scatter.47.cloned.1.call-done = bf16[240,2560]{1,0:T(8,128)(2,1)} async-done(((bf16[960,2560]{1,0:T(8,128)(2,1)}), bf16[240,2560]{1,0:T(8,128)(2,1)}) %reduce-scatter.47.cloned.1.call-update) | async-done | bytes 1228816 | tf_op jit(solution)/shard_map/reduce_scatter | solution.py:321
  1043.7 49.5 %reduce-scatter.61.cloned.1.call-done = bf16[640,960]{1,0:T(8,128)(2,1)} async-done(((bf16[2560,960]{1,0:T(8,128)(2,1)}), bf16[640,960]{1,0:T(8,128)(2,1)}) %reduce-scatter.61.cloned.1.call-update) | async-done | bytes 1228816
  1095.6 6.5 add_convert_fusion
  1108.7 47.3 %reduce-scatter.49.cloned.1.call-done = bf16[120,240]{1,0:T(8,128)(2,1)} async-done(((bf16[960,240]{1,0:T(8,128)(2,1)}), bf16[120,240]{1,0:T(8,128)(2,1)}) %reduce-scatter.49.cloned.1.call-update) | async-done | bytes 57616
  1157.6 60.4 %reduce-scatter.55.cloned.1.call-done = bf16[120,240]{1,0:T(8,128)(2,1)} async-done(((bf16[960,240]{1,0:T(8,128)(2,1)}), bf16[120,240]{1,0:T(8,128)(2,1)}) %reduce-scatter.55.cloned.1.call-update) | async-done | bytes 57616
  1231.3 6.0 all-reduce.6
  1237.5 19.7 %all-reduce.5 = (f32[240]{0:T(256)}, f32[240]{0:T(256)}) all-reduce(f32[240]{0:T(256)S(1)} %get-tuple-element.331, f32[240]{0:T(256)S(1)} %get-tuple-element.330), channel_id=1, replica_groups=mesh['ctx'=8,'fsdp'=4] {'ctx'}, use_global_device_ids=true, to_apply=%region_15.16 | all-reduce | flops 480 | bytes 3840 | tf_op jit(solution)/shard_map/psum | solution.py:351
  1257.1 18.3 %reduce-scatter.39.cloned.1.call-done = bf16[240,40]{0,1:T(8,128)(2,1)} async-done(((bf16[240,320]{0,1:T(8,128)(2,1)}), bf16[240,40]{0,1:T(8,128)(2,1)}) %reduce-scatter.39.cloned.1.call-update) | async-done | bytes 19216 | tf_op jit(solution)/shard_map/reduce_scatter | solution.py:332
  1276.8 55.9 %reduce-scatter.41.cloned.1.call-done = bf16[240,40]{0,1:T(8,128)(2,1)} async-done(((bf16[240,320]{0,1:T(8,128)(2,1)}), bf16[240,40]{0,1:T(8,128)(2,1)}) %reduce-scatter.41.cloned.1.call-update) | async-done | bytes 19216 | tf_op jit(solution)/shard_map/reduce_scatter | solution.py:335
  1334.1 65.8 %reduce-scatter.57.cloned.1.call-done = bf16[320,240]{1,0:T(8,128)(2,1)} async-done(((bf16[2560,240]{1,0:T(8,128)(2,1)}), bf16[320,240]{1,0:T(8,128)(2,1)}) %reduce-scatter.57.cloned.1.call-update) | async-done | bytes 153616
  1401.8 65.1 %reduce-scatter.59.cloned.1.call-done = bf16[320,240]{1,0:T(8,128)(2,1)} async-done(((bf16[2560,240]{1,0:T(8,128)(2,1)}), bf16[320,240]{1,0:T(8,128)(2,1)}) %reduce-scatter.59.cloned.1.call-update) | async-done | bytes 153616
  1468.9 63.4 %reduce-scatter.63.cloned.1.call-done = bf16[640,120]{0,1:T(8,128)(2,1)} async-done(((bf16[640,960]{0,1:T(8,128)(2,1)}), bf16[640,120]{0,1:T(8,128)(2,1)}) %reduce-scatter.63.cloned.1.call-update) | async-done | bytes 153616
  (645 shorter events, 420.7 us)
Async XLA Ops:
  7.2 26.4 %copy-start.3 = (bf16[4,1,2,64,960]{4,3,2,1,0:T(8,128)(2,1)S(1)}, bf16[4,1,2,64,960]{4,3,2,1,0:T(8,128)(2,1)}, u32[]{:S(2)}) copy-start(bf16[4,1,2,64,960]{4,3,2,1,0:T(8,128)(2,1)} %param.16) | copy-start | bytes 2949124
  7.2 49.9 %all-gather.10.cloned.1.call-start = ((), (), s32[]{:S(2)}) async-start(), calls=%async_computation.16 | async-start | bytes 2457600 | tf_op jit(solution)/shard_map/all_gather | solution.py:118
  7.9 92.5 %all-gather.12.cloned.1.call-start = ((), (), s32[]{:S(2)}) async-start(), calls=%async_computation.17 | async-start | bytes 3538944 | tf_op jit(solution)/shard_map/all_gather | solution.py:142
  20.0 29.7 %copy-start.29 = (f32[960]{0:T(1024)}, f32[960]{0:T(1024)S(1)}, u32[]{:S(2)}) copy-start(f32[960]{0:T(1024)S(1)} %convert_element_type.202) | copy-start | bytes 11524
  33.5 1.8 copy-start.22
  34.4 29.7 %copy-start.11 = (f32[512,64]{0,1:T(8,128)}, f32[512,64]{0,1:T(8,128)S(1)}, u32[]{:S(2)}) copy-start(f32[512,64]{0,1:T(8,128)S(1)} %get-tuple-element.320) | copy-start | bytes 393220
  34.4 29.7 %copy-start.19 = (f32[512,64]{0,1:T(8,128)}, f32[512,64]{0,1:T(8,128)S(1)}, u32[]{:S(2)}) copy-start(f32[512,64]{0,1:T(8,128)S(1)} %get-tuple-element.321) | copy-start | bytes 393220
  37.6 124.1 %all-gather.14.cloned.1.call-start = ((), (), s32[]{:S(2)}) async-start(), calls=%async_computation.18 | async-start | bytes 3538944 | tf_op jit(solution)/shard_map/all_gather | solution.py:143
  37.7 12.0 copy-start.31
  51.3 222.4 %all-gather.16.cloned.1.call-start = ((), (), s32[]{:S(2)}) async-start(), calls=%async_computation.19 | async-start | bytes 2457600 | tf_op jit(solution)/shard_map/all_gather | solution.py:121
  51.9 227.2 %all-gather.18.cloned.1.call-start = ((), (), s32[]{:S(2)}) async-start(), calls=%async_computation.20 | async-start | bytes 6144000 | tf_op jit(solution)/shard_map/all_gather | solution.py:203
  52.5 3.2 copy-start.26
  52.5 234.0 %all-gather.20.cloned.1.call-start = ((), (), s32[]{:S(2)}) async-start(), calls=%async_computation.21 | async-start | bytes 6144000 | tf_op jit(solution)/shard_map/all_gather | solution.py:204
  53.1 250.9 %all-gather.22.cloned.1.call-start = ((), (), s32[]{:S(2)}) async-start(), calls=%async_computation.22 | async-start | bytes 6144000 | tf_op jit(solution)/shard_map/all_gather | solution.py:205
  53.8 643.9 %reduce-scatter.33.cloned.1.call-start = ((), (), s32[]{:S(2)}) async-start(), calls=%async_computation.23 | async-start | bytes 7077888 | tf_op jit(solution)/shard_map/reduce_scatter | solution.py:253
  57.1 3.9 copy-start.5
  173.3 12.3 copy-start.18
  272.0 5.5 copy-start.35
  279.1 7.4 copy-start.1
  313.9 6.6 copy-start.37
  313.9 6.6 copy-start.36
  313.9 6.6 copy-start.10
  314.0 6.6 copy-start.16
  320.6 3.7 copy-start.17
  324.2 1.9 copy-start.34
  579.6 238.9 %reduce-scatter.35.cloned.1.call-start = ((), (), s32[]{:S(2)}) async-start(), calls=%async_computation.24 | async-start | bytes 7077888 | tf_op jit(solution)/shard_map/reduce_scatter | solution.py:254
  605.5 247.7 %reduce-scatter.37.cloned.1.call-start = ((), (), s32[]{:S(2)}) async-start(), calls=%async_computation.25 | async-start | bytes 2457600 | tf_op jit(solution)/shard_map/reduce_scatter | solution.py:306
  609.7 3.2 copy-start.20
  616.2 2.0 copy-start.6
  620.9 263.2 %reduce-scatter.43.cloned.1.call-start = ((), (), s32[]{:S(2)}) async-start(), calls=%async_computation.28 | async-start | bytes 2457600 | tf_op jit(solution)/shard_map/reduce_scatter | solution.py:315
  625.4 284.1 %reduce-scatter.51.cloned.1.call-start = ((), (), s32[]{:S(2)}) async-start(), calls=%async_computation.32 | async-start | bytes 921600
  709.6 226.2 %reduce-scatter.53.cloned.1.call-start = ((), (), s32[]{:S(2)}) async-start(), calls=%async_computation.33 | async-start | bytes 921600
  819.7 5.0 copy-start.2
  824.7 162.8 %reduce-scatter.45.cloned.1.call-start = ((), (), s32[]{:S(2)}) async-start(), calls=%async_computation.29 | async-start | bytes 6144000 | tf_op jit(solution)/shard_map/reduce_scatter | solution.py:318
  831.0 208.3 %reduce-scatter.47.cloned.1.call-start = ((), (), s32[]{:S(2)}) async-start(), calls=%async_computation.30 | async-start | bytes 6144000 | tf_op jit(solution)/shard_map/reduce_scatter | solution.py:321
  837.4 255.8 %reduce-scatter.61.cloned.1.call-start = ((), (), s32[]{:S(2)}) async-start(), calls=%async_computation.37 | async-start | bytes 6553600
  853.1 302.9 %reduce-scatter.49.cloned.1.call-start = ((), (), s32[]{:S(2)}) async-start(), calls=%async_computation.31 | async-start | bytes 552960
  855.2 362.7 %reduce-scatter.55.cloned.1.call-start = ((), (), s32[]{:S(2)}) async-start(), calls=%async_computation.34 | async-start | bytes 552960
  886.2 389.3 %reduce-scatter.39.cloned.1.call-start = ((), (), s32[]{:S(2)}) async-start(), calls=%async_computation.26 | async-start | bytes 184320 | tf_op jit(solution)/shard_map/reduce_scatter | solution.py:332
  911.2 421.5 %reduce-scatter.41.cloned.1.call-start = ((), (), s32[]{:S(2)}) async-start(), calls=%async_computation.27 | async-start | bytes 184320 | tf_op jit(solution)/shard_map/reduce_scatter | solution.py:335
  937.5 462.4 %reduce-scatter.57.cloned.1.call-start = ((), (), s32[]{:S(2)}) async-start(), calls=%async_computation.35 | async-start | bytes 1474560
  989.9 477.1 %reduce-scatter.59.cloned.1.call-start = ((), (), s32[]{:S(2)}) async-start(), calls=%async_computation.36 | async-start | bytes 1474560
  1041.7 1.9 copy-start.32
  1041.7 490.5 %reduce-scatter.63.cloned.1.call-start = ((), (), s32[]{:S(2)}) async-start(), calls=%async_computation.38 | async-start | bytes 1382400
  1103.4 2.9 copy-start.24
  1108.7 113.1 %copy-start.21 = (f32[4,1,2,64,320]{4,3,2,0,1:T(8,128)S(1)}, f32[4,1,2,64,320]{4,3,2,0,1:T(8,128)}, u32[]{:S(2)}) copy-start(f32[4,1,2,64,320]{4,3,2,0,1:T(8,128)} %reduce-scatter.33.cloned.1.call-done) | copy-start | bytes 1966084
  1223.4 1.8 copy-start.25
  1228.4 2.9 copy-start.33
  (13 other events, 17.6 us)
Sparse Core Ops, SparseCore 0:
  9.6 28.0 all-gather.9
  39.9 60.4 all-gather.11
  102.6 59.0 all-gather.13
  163.1 20.4 all-gather.15
  185.0 38.7 all-gather.17
  225.2 38.5 all-gather.19
  265.4 38.5 all-gather.21
  579.7 117.9 reduce-scatter.32
  701.3 117.1 reduce-scatter.34
  820.9 29.7 reduce-scatter.36
  853.4 30.6 reduce-scatter.42
  886.5 22.9 reduce-scatter.50
  912.8 22.9 reduce-scatter.52
  938.2 49.1 reduce-scatter.44
  990.1 49.1 reduce-scatter.46
  1041.7 51.3 reduce-scatter.60
  1096.7 59.2 reduce-scatter.48
  1159.5 58.4 reduce-scatter.54
  1222.0 53.3 reduce-scatter.38
  1279.3 53.3 reduce-scatter.40
  1336.5 63.3 reduce-scatter.56
  1403.7 63.2 reduce-scatter.58
  1470.8 61.3 reduce-scatter.62
where the time goes:
time: 1550 us; the launch traced here: 1540 us
  waiting for transfers between devices  866 us (56%)
  matrix products  312 us (20%)
  local copies, waits for them, and re-layouts  216 us (14%)
  other arithmetic  75.3 us (5%)
  blocking collectives  53.6 us (3%)
  between operations  16.2 us (1%)
    unnamed x31, waiting for transfers between devices  403 us
    reduce_scatter x1, waiting for transfers between devices, shards(): lax.psum_scatter(unhead(value_back), 'ctx', scatter_dimension=1, tiled=True)  109 us
    reduce_scatter x1, waiting for transfers between devices, shards(): lax.psum_scatter(unhead(key_back), 'ctx', scatter_dimension=1, tiled=True)  72.2 us
    dot_general x40, matrix products, score_block(): jnp.einsum('gqd,kd->gqk', query_part, key_part, preferred_element_type=jn...  62.9 us
    reduce_scatter x1, waiting for transfers between devices, shards(): lax.psum_scatter(value_grad.astype(jnp.bfloat16), 'ctx', scatter_dimensio...  55.9 us
    reshape x4, local copies, waits for them, and re-layouts, unhead(): return value_rows.reshape(sequence_batch, KEY_VALUE_HEADS, key_rows_total...  51.2 us
    reduce_scatter x1, waiting for transfers between devices, shards(): lax.psum_scatter(gate_grad.astype(jnp.bfloat16), 'fsdp', scatter_dimensio...  49.9 us
    reduce_scatter x1, waiting for transfers between devices, shards(): lax.psum_scatter(up_grad.astype(jnp.bfloat16), 'fsdp', scatter_dimension=...  49.4 us
  transfers between devices with their start and end apart: 23, of which 18 were waited for; matrix products, arithmetic and copies ran while one was open for 21% of the time, Pallas kernels for 0%

commit v1 on v0

v1 whole, which is shorter than its diff:
```python
import functools

import jax
import jax.numpy as jnp
from jax import lax
from jax.experimental import pallas as pl
from jax.experimental.pallas import tpu as pltpu
from jax.sharding import PartitionSpec as P

QUERY_HEADS = 15
KEY_VALUE_HEADS = 5
HEAD_SIZE = 64
GROUP = QUERY_HEADS // KEY_VALUE_HEADS
KV = KEY_VALUE_HEADS * HEAD_SIZE
SCALE = HEAD_SIZE**-0.5
VMEM = 50 * 1024 * 1024

eps = 1e-05
theta_base = 100000.0
bf16, f32 = jnp.bfloat16, jnp.float32


def dot(left, right, contract=((1,), (0,))):
    return lax.dot_general(left, right, (contract, ((), ())), preferred_element_type=f32)


NT = ((1,), (1,))
TN = ((0,), (0,))


def query_quarter(half, member, quarters):
    return jnp.where(half == 0, member, quarters - 1 - member)


def split_heads(source, target, half_rows):
    for half in range(2):
        rows = slice(half * half_rows, (half + 1) * half_rows)
        for g in range(KEY_VALUE_HEADS):
            for i in range(GROUP):
                lane = (g * GROUP + i) * HEAD_SIZE
                yield half, g, slice(i * half_rows, (i + 1) * half_rows), rows, slice(
                    lane, lane + HEAD_SIZE
                )


def diagonal_mask(tq):
    key_at = lax.broadcasted_iota(jnp.int32, (tq, GROUP * tq), 0)
    query_at = lax.broadcasted_iota(jnp.int32, (tq, GROUP * tq), 1) % tq
    return key_at <= query_at


def forward_kernel(member_ref, q_ref, kv_ref, mixed_ref, lse_ref, qh, top_s, sum_s, acc_s):
    tq = q_ref.shape[0] // 2
    quarters = kv_ref.shape[0] // tq
    member = member_ref[0]
    for half, g, hr, rows, lanes in split_heads(q_ref, qh, tq):
        qh[half, g, hr, :] = q_ref[rows, lanes] * jnp.asarray(SCALE, bf16)

    def one_half(half, _):
        own = query_quarter(half, member, quarters)

        def tile(ki, first):
            rows = pl.ds(pl.multiple_of(ki * tq, tq), tq)
            for g in range(KEY_VALUE_HEADS):
                keys = kv_ref[rows, g * HEAD_SIZE : (g + 1) * HEAD_SIZE]
                values = kv_ref[rows, KV + g * HEAD_SIZE : KV + (g + 1) * HEAD_SIZE]
                scores = dot(keys, qh[half, g], NT)
                if first:
                    scores = jnp.where(diagonal_mask(tq), scores, -1e30)
                    top = jnp.max(scores, axis=0, keepdims=True)
                    weights = jnp.exp(scores - top)
                    sum_s[g] = jnp.sum(weights, axis=0, keepdims=True)
                    acc_s[g] = dot(values, weights.astype(bf16), TN)
                else:
                    before = top_s[g]
                    top = jnp.maximum(before, jnp.max(scores, axis=0, keepdims=True))
                    weights = jnp.exp(scores - top)
                    fade = jnp.exp(before - top)
                    sum_s[g] = sum_s[g] * fade + jnp.sum(weights, axis=0, keepdims=True)
                    acc_s[g] = acc_s[g] * fade + dot(values, weights.astype(bf16), TN)
                top_s[g] = top

        tile(own, True)

        def body(ki, _):
            tile(ki, False)
            return 0

        lax.fori_loop(0, own, body, 0)
        rows = pl.ds(pl.multiple_of(half * tq, tq), tq)
        for g in range(KEY_VALUE_HEADS):
            total = sum_s[g]
            mixed = (acc_s[g] / total).T
            lse_ref[half, g] = top_s[g] + jnp.log(total)
            for i in range(GROUP):
                lane = (g * GROUP + i) * HEAD_SIZE
                mixed_ref[rows, lane : lane + HEAD_SIZE] = mixed[i * tq : (i + 1) * tq].astype(bf16)
        return 0

    lax.fori_loop(0, 2, one_half, 0)


def attention_forward(member, query, kv):
    rows, width = query.shape
    tq = rows // 2
    vm = pl.BlockSpec(memory_space=pltpu.VMEM)
    row = (KEY_VALUE_HEADS, 1, GROUP * tq)
    flops = 4 * 5 * tq * tq * width
    return pl.pallas_call(
        forward_kernel,
        out_shape=(
            jax.ShapeDtypeStruct((rows, width), bf16),
            jax.ShapeDtypeStruct((2,) + row, f32),
        ),
        in_specs=[pl.BlockSpec(memory_space=pltpu.SMEM), vm, vm],
        out_specs=(vm, vm),
        scratch_shapes=[
            pltpu.VMEM((2, KEY_VALUE_HEADS, GROUP * tq, HEAD_SIZE), bf16),
            pltpu.VMEM(row, f32),
            pltpu.VMEM(row, f32),
            pltpu.VMEM((KEY_VALUE_HEADS, HEAD_SIZE, GROUP * tq), f32),
        ],
        compiler_params=pltpu.CompilerParams(vmem_limit_bytes=VMEM),
        cost_estimate=pl.CostEstimate(
            flops=flops * 8, bytes_accessed=4 * rows * width, transcendentals=flops // 256
        ),
        name="attention_forward",
    )(member, query, kv)


def backward_kernel(
    member_ref, q_ref, kv_ref, mixed_ref, grad_ref, lse_ref, dq_ref, dkv_ref, qh, gh, delta, dq_s, dk_s, dv_s
):
    tq = q_ref.shape[0] // 2
    quarters = kv_ref.shape[0] // tq
    member = member_ref[0]
    ones = jnp.ones((8, HEAD_SIZE), bf16)
    for half, g, hr, rows, lanes in split_heads(q_ref, qh, tq):
        qh[half, g, hr, :] = q_ref[rows, lanes] * jnp.asarray(SCALE, bf16)
        grads = grad_ref[rows, lanes]
        gh[half, g, hr, :] = grads
        product = grads.astype(f32) * mixed_ref[rows, lanes].astype(f32)
        high = product.astype(bf16)
        low = (product - high.astype(f32)).astype(bf16)
        delta[half, g, :, hr] = (dot(ones, high, NT) + dot(ones, low, NT))[0:1]
    dk_s[...] = jnp.zeros_like(dk_s)
    dv_s[...] = jnp.zeros_like(dv_s)

    def one_half(half, _):
        own = query_quarter(half, member, quarters)

        def tile(ki, first):
            rows = pl.ds(pl.multiple_of(ki * tq, tq), tq)
            for g in range(KEY_VALUE_HEADS):
                keys = kv_ref[rows, g * HEAD_SIZE : (g + 1) * HEAD_SIZE]
                values = kv_ref[rows, KV + g * HEAD_SIZE : KV + (g + 1) * HEAD_SIZE]
                query = qh[half, g]
                grads = gh[half, g]
                probs = jnp.exp(dot(keys, query, NT) - lse_ref[half, g])
                if first:
                    probs = jnp.where(diagonal_mask(tq), probs, 0.0)
                grad_probs = dot(values, grads, NT)
                dv_s[g, rows, :] += dot(probs.astype(bf16), grads)
                grad_scores = (probs * (grad_probs - delta[half, g])).astype(bf16)
                dk_s[g, rows, :] += dot(grad_scores, query)
                dq = dot(keys, grad_scores, TN)
                if first:
                    dq_s[g] = dq
                else:
                    dq_s[g] += dq

        tile(own, True)

        def body(ki, _):
            tile(ki, False)
            return 0

        lax.fori_loop(0, own, body, 0)
        rows = pl.ds(pl.multiple_of(half * tq, tq), tq)
        for g in range(KEY_VALUE_HEADS):
            dq = (dq_s[g] * SCALE).T
            for i in range(GROUP):
                lane = (g * GROUP + i) * HEAD_SIZE
                dq_ref[rows, lane : lane + HEAD_SIZE] = dq[i * tq : (i + 1) * tq]
        return 0

    lax.fori_loop(0, 2, one_half, 0)
    for g in range(KEY_VALUE_HEADS):
        dkv_ref[:, g * HEAD_SIZE : (g + 1) * HEAD_SIZE] = dk_s[g]
        dkv_ref[:, KV + g * HEAD_SIZE : KV + (g + 1) * HEAD_SIZE] = dv_s[g]


def attention_backward(member, query, kv, mixed, grad_mixed, lse):
    rows, width = query.shape
    tq = rows // 2
    vm = pl.BlockSpec(memory_space=pltpu.VMEM)
    heads = (2, KEY_VALUE_HEADS, GROUP * tq, HEAD_SIZE)
    flops = 10 * 5 * tq * tq * width
    return pl.pallas_call(
        backward_kernel,
        out_shape=(
            jax.ShapeDtypeStruct((rows, width), f32),
            jax.ShapeDtypeStruct(kv.shape, f32),
        ),
        in_specs=[pl.BlockSpec(memory_space=pltpu.SMEM)] + [vm] * 5,
        out_specs=(vm, vm),
        scratch_shapes=[
            pltpu.VMEM(heads, bf16),
            pltpu.VMEM(heads, bf16),
            pltpu.VMEM((2, KEY_VALUE_HEADS, 1, GROUP * tq), f32),
            pltpu.VMEM((KEY_VALUE_HEADS, HEAD_SIZE, GROUP * tq), f32),
            pltpu.VMEM((KEY_VALUE_HEADS, kv.shape[0], HEAD_SIZE), f32),
            pltpu.VMEM((KEY_VALUE_HEADS, kv.shape[0], HEAD_SIZE), f32),
        ],
        compiler_params=pltpu.CompilerParams(vmem_limit_bytes=VMEM),
        cost_estimate=pl.CostEstimate(
            flops=flops * 8, bytes_accessed=12 * rows * width, transcendentals=flops // 640
        ),
        name="attention_backward",
    )(member, query, kv, mixed, grad_mixed, lse)


def rope_tables(positions):
    half = HEAD_SIZE // 2
    freqs = theta_base ** (-jnp.arange(half, dtype=f32) * 2.0 / HEAD_SIZE)
    angles = positions[:, None] * freqs
    cosine, sine = jnp.cos(angles), jnp.sin(angles)
    return jnp.concatenate([cosine, cosine], axis=1), jnp.concatenate([sine, sine], axis=1)


def rotate(rows):
    half = HEAD_SIZE // 2
    width = rows.shape[1]
    ahead = jnp.concatenate([rows[:, half:], rows[:, :half]], axis=1)
    behind = jnp.concatenate([rows[:, width - half :], rows[:, : width - half]], axis=1)
    lane = lax.broadcasted_iota(jnp.int32, rows.shape, 1) % HEAD_SIZE
    return jnp.where(lane < half, -ahead, behind)


def widen(table, width):
    return jnp.concatenate([table] * (width // HEAD_SIZE), axis=1)


def rotate_pairs(rows, cosine, sine):
    width = rows.shape[1]
    return rows * widen(cosine, width) + rotate(rows) * widen(sine, width)


def rotate_pairs_back(grads, cosine, sine):
    width = grads.shape[1]
    return grads * widen(cosine, width) - rotate(grads * widen(sine, width))


def norm_forward(rows, gain):
    inverse = lax.rsqrt(jnp.mean(rows * rows, axis=-1, keepdims=True) + eps)
    return rows * inverse * gain, inverse


def norm_backward(rows, inverse, gain, grad_normed):
    scaled = grad_normed * gain
    gain_grad = jnp.sum(grad_normed * rows * inverse, axis=0)
    value_grad = inverse * scaled - rows * inverse**3 * jnp.mean(
        scaled * rows, axis=-1, keepdims=True
    )
    return value_grad, gain_grad


class Layout:
    def __init__(self, seqs):
        self.S = seqs
        self.Pn = lax.axis_size("ctx")
        self.F = lax.axis_size("fsdp")
        self.places = self.Pn // (2 * seqs)
        self.G = 2 * self.places
        self.t = lax.axis_index("ctx")
        self.f = lax.axis_index("fsdp")
        core = self.f % 2
        self.member = (self.t % self.places) * 2 + core
        self.sequence = (self.t // self.places) % seqs

    def spread(self, r):
        pairs = []
        for u in range(self.Pn):
            for f in range(self.F):
                s = (u % self.S + r) % self.S
                m = u // self.S
                t = ((f % 2) * self.S + s) * self.places + m // 2
                pairs.append((u * self.F + f, t * self.F + (f // 2) * 2 + m % 2))
        return pairs

    def ring(self, r):
        pairs = []
        for t in range(self.Pn):
            for f in range(self.F):
                base = t - t % self.places
                m = ((t % self.places) * 2 + f % 2 + r) % self.G
                pairs.append((t * self.F + f, (base + m // 2) * self.F + (f // 2) * 2 + m % 2))
        return pairs

    def to_sequence(self, array):
        got = []
        for r in range(self.S):
            piece = lax.dynamic_index_in_dim(
                array, (self.t % self.S + r) % self.S, 0, keepdims=False
            )
            got.append(lax.ppermute(piece, ("ctx", "fsdp"), self.spread(r)))
        ordered = jnp.stack(got[::-1] + got[::-1])
        start = (self.S - 1 - self.sequence) % self.S
        ordered = lax.dynamic_slice_in_dim(ordered, start, self.S, 0)
        low, high = ordered[:, 0], ordered[::-1, 1]
        block, width = array.shape[2], array.shape[3]
        return jnp.concatenate(
            [low.reshape(self.S * block, width), high.reshape(self.S * block, width)], axis=0
        )

    def from_sequence(self, rows):
        width = rows.shape[1]
        block = rows.shape[0] // (2 * self.S)
        halves = rows.reshape(2, self.S, block, width)
        array = jnp.stack([halves[0], halves[1, ::-1]], axis=1)
        got = []
        for r in range(self.S):
            piece = lax.dynamic_index_in_dim(
                array, (self.sequence - r + self.S) % self.S, 0, keepdims=False
            )
            back = [(b, a) for a, b in self.spread(r)]
            got.append(lax.ppermute(piece, ("ctx", "fsdp"), back))
        ordered = jnp.stack(got + got)
        start = (self.S - self.t % self.S) % self.S
        return lax.dynamic_slice_in_dim(ordered, start, self.S, 0)

    def gather_group(self, rows):
        tq, width = rows.shape[0] // 2, rows.shape[1]
        got = [rows] + [
            lax.ppermute(rows, ("ctx", "fsdp"), self.ring(r)) for r in range(1, self.G)
        ]
        got = [g.reshape(2, tq, width) for g in got]
        if self.G == 2:
            even = self.member == 0
            first, second = jnp.where(even, got[0], got[1]), jnp.where(even, got[1], got[0])
            whole = jnp.stack([first[0], second[0], second[1], first[1]])
        else:
            ordered = jnp.stack(got[::-1] + got[::-1])
            ordered = lax.dynamic_slice_in_dim(ordered, (self.G - 1 - self.member), self.G, 0)
            whole = jnp.concatenate([ordered[:, 0], ordered[::-1, 1]])
        return whole.reshape(2 * self.G * tq, width)

    def scatter_group(self, rows):
        quarters = 2 * self.G
        tq, width = rows.shape[0] // quarters, rows.shape[1]
        parts = rows.reshape(quarters, tq, width)

        def of(m):
            low = lax.dynamic_index_in_dim(parts, m, 0, keepdims=False)
            high = lax.dynamic_index_in_dim(parts, quarters - 1 - m, 0, keepdims=False)
            return jnp.concatenate([low, high])

        total = of(self.member)
        for r in range(1, self.G):
            piece = of((self.member + r) % self.G).astype(bf16)
            total = total + lax.ppermute(piece, ("ctx", "fsdp"), self.ring(r)).astype(f32)
        return total


def swap(array, axis, bit):
    size = lax.axis_size(axis)
    return lax.ppermute(array, axis, [(i, i ^ bit) for i in range(size)])


def choose(flag, one, other):
    return jnp.where(flag, one, other)


def gather_halves(low, high):
    f, y = lax.axis_index("fsdp"), lax.axis_index("ctx") % 2
    crossed = swap(choose(y == 0, low, high), "fsdp", 2)
    passed = swap(crossed, "ctx", 1)
    far_low, far_high = choose(y == 0, crossed, passed), choose(y == 0, passed, crossed)
    out = []
    for near, far in ((low, far_low), (high, far_high)):
        other = swap(jnp.stack([near, far]), "fsdp", 1)
        rows = near.shape[0]
        full = jnp.zeros((4 * rows, near.shape[1]), near.dtype)
        for piece, place in ((near, f), (far, f ^ 2), (other[0], f ^ 1), (other[1], f ^ 3)):
            full = lax.dynamic_update_slice_in_dim(full, piece, place * rows, 0)
        out.append(full)
    return out


def scatter_sum(grads, cols):
    f, t = lax.axis_index("fsdp"), lax.axis_index("ctx")
    rows = grads.shape[0] // 4
    core, x, y, z = f % 2, f // 2, t % 2, t // 2

    def add(one, other):
        return (one.astype(f32) + other.astype(f32)).astype(bf16)

    parts = grads.reshape(2, 2, rows, grads.shape[1])
    even, odd = parts[:, 0], parts[:, 1]
    both = add(choose(core == 0, even, odd), swap(choose(core == 0, odd, even), "fsdp", 1))
    half = add(choose(x == 0, both[0], both[1]), swap(choose(x == 0, both[1], both[0]), "fsdp", 2))
    places = [half[:, i * cols : (i + 1) * cols] for i in range(8)]
    even, odd = jnp.stack(places[0::2]), jnp.stack(places[1::2])
    line = add(choose(y == 0, even, odd), swap(choose(y == 0, odd, even), "ctx", 1))

    def own(k):
        return lax.dynamic_index_in_dim(line, jnp.clip(k, 0, 3), 0, keepdims=False)

    up = down = None
    for step in range(1, 4):
        send_up, send_down = own(z + 4 - step), own(z - 4 + step)
        if step > 1:
            send_up, send_down = add(send_up, up), add(send_down, down)
        ups = [(2 * k + j, 2 * k + 2 + j) for k in range(step) for j in range(2)]
        downs = [(2 * (3 - k) + j, 2 * (3 - k) - 2 + j) for k in range(step) for j in range(2)]
        up, down = lax.ppermute(send_up, "ctx", ups), lax.ppermute(send_down, "ctx", downs)
    return own(z).astype(f32) + up.astype(f32) + down.astype(f32)


def shards(
    inputs,
    attn_gain,
    query_weight,
    key_projection_weight,
    value_projection_weight,
    out_weight,
    ffn_gain,
    gate_weight,
    up_weight,
    down_weight,
    positions,
    cotangent,
):
    seqs, _, _, block, width = inputs.shape
    lay = Layout(seqs)
    fast = lay.F == 4 and lay.Pn == 8
    ff = gate_weight.shape[1]

    place = positions.reshape(seqs, 2, block, 1)
    packed = jnp.concatenate(
        [
            inputs.reshape(seqs, 2, block, width),
            (place // 128).astype(bf16),
            (place % 128).astype(bf16),
        ],
        axis=-1,
    )
    packed = lay.to_sequence(packed)
    residual = packed[:, :width].astype(f32)
    place = packed[:, width].astype(f32) * 128.0 + packed[:, width + 1].astype(f32)
    member = lay.member.astype(jnp.int32).reshape(1)

    gains = lax.all_gather(jnp.stack([attn_gain, ffn_gain]), "fsdp", axis=1, tiled=True)
    gains = gains.astype(f32)
    first_gain, second_gain = gains[0], gains[1]
    if fast:
        attn_low = jnp.concatenate([query_weight, key_projection_weight], axis=1)
        attn_high = jnp.concatenate([value_projection_weight, out_weight], axis=1)
        low, high = gather_halves(attn_low, attn_high)
        query_full, key_full = low[:, :width], low[:, width:]
        value_full, out_full = high[:, :KV], high[:, KV:]
        gate_full, up_full = gather_halves(gate_weight, up_weight)
        rows = down_weight.shape[0] // 2
        down_low, down_high = gather_halves(down_weight[:rows], down_weight[rows:])
        down_full = jnp.stack(
            [down_low.reshape(4, rows, width), down_high.reshape(4, rows, width)], axis=1
        ).reshape(ff, width)
    else:
        query_full, key_full, value_full, out_full, gate_full, up_full, down_full = [
            lax.all_gather(w, "fsdp", axis=0, tiled=True)
            for w in (
                query_weight,
                key_projection_weight,
                value_projection_weight,
                out_weight,
                gate_weight,
                up_weight,
                down_weight,
            )
        ]

    cosine, sine = rope_tables(place)
    normalized, inverse_first = norm_forward(residual, first_gain)
    normed = normalized.astype(bf16)
    query = rotate_pairs(dot(normed, query_full), cosine, sine).astype(bf16)
    keys = rotate_pairs(dot(normed, key_full), cosine, sine).astype(bf16)
    values = dot(normed, value_full).astype(bf16)
    kv = lay.gather_group(jnp.concatenate([keys, values], axis=1))
    mixed, lse = attention_forward(member, query, kv)
    hidden = residual + dot(mixed, out_full)

    grad_rows = lay.to_sequence(cotangent.reshape(seqs, 2, block, width))
    normed_ffn, inverse_second = norm_forward(hidden, second_gain)
    normed_ffn = normed_ffn.astype(bf16)
    gate = dot(normed_ffn, gate_full)
    up_part = dot(normed_ffn, up_full)
    sigmoid = jax.nn.sigmoid(gate)
    act = (gate * sigmoid * up_part).astype(bf16)
    outputs = lay.from_sequence((hidden + dot(act, down_full)).astype(bf16))
    down_grad = dot(act, grad_rows, TN).astype(bf16)
    grad_act = dot(grad_rows, down_full, NT)
    grad_up = (grad_act * gate * sigmoid).astype(bf16)
    grad_gate = (grad_act * up_part * sigmoid * (1.0 + gate * (1.0 - sigmoid))).astype(bf16)
    gate_grad = dot(normed_ffn, grad_gate, TN).astype(bf16)
    up_grad = dot(normed_ffn, grad_up, TN).astype(bf16)
    grad_normed_ffn = dot(grad_gate, gate_full, NT) + dot(grad_up, up_full, NT)
    through, ffn_gain_grad = norm_backward(hidden, inverse_second, second_gain, grad_normed_ffn)
    grad_hidden = grad_rows.astype(f32) + through
    grad_branch = grad_hidden.astype(bf16)
    out_grad = dot(mixed, grad_branch, TN).astype(bf16)
    grad_mixed = dot(grad_branch, out_full, NT).astype(bf16)

    dq, dkv = attention_backward(member, query, kv, mixed, grad_mixed, lse)
    dkv = lay.scatter_group(dkv)
    grad_query = rotate_pairs_back(dq, cosine, sine).astype(bf16)
    grad_key = rotate_pairs_back(dkv[:, :KV], cosine, sine).astype(bf16)
    grad_value = dkv[:, KV:].astype(bf16)
    query_grad = dot(normed, grad_query, TN).astype(bf16)
    key_grad = dot(normed, grad_key, TN).astype(bf16)
    value_grad = dot(normed, grad_value, TN).astype(bf16)
    grad_normed = (
        dot(grad_query, query_full, NT) + dot(grad_key, key_full, NT) + dot(grad_value, value_full, NT)
    )
    grad_input, attn_gain_grad = norm_backward(residual, inverse_first, first_gain, grad_normed)
    input_grad = lay.from_sequence((grad_hidden + grad_input).astype(bf16)).astype(f32)

    def scatter(grads):
        cols = grads.shape[1] // lay.Pn
        if fast:
            return scatter_sum(grads, cols)
        part = lax.psum_scatter(grads, "fsdp", scatter_dimension=0, tiled=True)
        return lax.psum_scatter(part, "ctx", scatter_dimension=1, tiled=True).astype(f32)

    down_grad, gate_grad, up_grad, out_grad, query_grad, key_grad, value_grad = [
        scatter(g)
        for g in (down_grad, gate_grad, up_grad, out_grad, query_grad, key_grad, value_grad)
    ]
    gain_grads = lax.psum(jnp.stack([attn_gain_grad, ffn_gain_grad]), ("ctx", "fsdp"))
    gain_rows = attn_gain.shape[0]
    gain_grads = lax.dynamic_slice_in_dim(gain_grads, lay.f * gain_rows, gain_rows, 1)
    return (
        outputs.reshape(inputs.shape),
        input_grad.reshape(inputs.shape),
        gain_grads[0],
        query_grad,
        key_grad,
        value_grad,
        out_grad,
        gain_grads[1],
        gate_grad,
        up_grad,
        down_grad,
    )


def solution(mesh):
    in_specs = (
        P("fsdp", "ctx", None, None, None),
        P("fsdp"),
        P("fsdp", None),
        P("fsdp", None),
        P("fsdp", None),
        P("fsdp", None),
        P("fsdp"),
        P("fsdp", None),
        P("fsdp", None),
        P("fsdp", None),
        P("fsdp", "ctx", None, None),
        P("fsdp", "ctx", None, None, None),
    )
    out_specs = (
        P("fsdp", "ctx", None, None, None),
        P("fsdp", "ctx", None, None, None),
        P("fsdp"),
        P("fsdp", "ctx"),
        P("fsdp", "ctx"),
        P("fsdp", "ctx"),
        P("fsdp", "ctx"),
        P("fsdp"),
        P("fsdp", "ctx"),
        P("fsdp", "ctx"),
        P("fsdp", "ctx"),
    )
    return jax.shard_map(shards, mesh=mesh, in_specs=in_specs, out_specs=out_specs, check_vma=False)
```

time: 1550 us -> 718 us (0.46)
  waiting for transfers between devices: 866 us -> 143 us
  matrix products: 312 us -> 74.6 us
  starting transfers between devices: 1.4 us -> 190 us
  local copies, waits for them, and re-layouts: 216 us -> 126 us
  Pallas kernels: 0 us -> 34.7 us
  other arithmetic: 75.3 us -> 93.5 us
    unnamed x31 -> x0, waiting for transfers between devices: 403 us -> none
    reduce_scatter x8 -> x0, waiting for transfers between devices: 383 us -> none  [the longest x1 109 us: shards(): lax.psum_scatter(unhead(value_back), 'ctx', scatter_dimension=1, tiled=True)]
    dot_general x161 -> x21, matrix products: 312 us -> 74.6 us  [dot(): lax.dot_general(left, right, (contract, ((), ())), preferred_element_type...]
    ppermute x0 -> x93, starting transfers between devices: none -> 190 us  [the longest x21 95.9 us: scatter_sum(): lax.ppermute(send_up, 'ctx', ups)]
    ppermute x0 -> x93, waiting for transfers between devices: none -> 143 us  [the longest x33 97.4 us: swap(): return lax.ppermute(array, axis, [(i, i ^ bit) for i in range(size)])]
    all_gather x7 -> x0, waiting for transfers between devices: 79.9 us -> none  [the longest x1 37.5 us: shards(): lax.all_gather(value_low, 'ctx', axis=1, tiled=True)]
    reshape x14 -> x4, local copies, waits for them, and re-layouts: 92.4 us -> 19.9 us  [the longest x3 18.9 us: scatter_sum(): parts = grads.reshape(2, 2, rows, grads.shape[1])]
    pallas_call x0 -> x2, Pallas kernels: none -> 34.7 us  [the longest x1 21 us: attention_backward(): pl.pallas_call(backward_kernel, out_shape=(jax.ShapeDtypeStruct((rows, wi...]
  transfers between devices with their start and end apart: 23 -> 93, of which waited for: 18 -> 26; matrix products, arithmetic and copies ran while one was open for 21% -> 31% of each run, Pallas kernels for 0% -> 2%
where the time goes in v1:
time: 718 us; the launch traced here: 710 us
  starting transfers between devices  190 us (26%)
  waiting for transfers between devices  143 us (20%)
  local copies, waits for them, and re-layouts  126 us (18%)
  other arithmetic  93.5 us (13%)
  matrix products  74.6 us (10%)
  blocking collectives  45.1 us (6%)
  Pallas kernels  34.7 us (5%)
    ppermute x33, waiting for transfers between devices, swap(): return lax.ppermute(array, axis, [(i, i ^ bit) for i in range(size)])  97.4 us
    ppermute x21, starting transfers between devices, scatter_sum(): lax.ppermute(send_up, 'ctx', ups)  95.9 us
    dot_general x21, matrix products, dot(): lax.dot_general(left, right, (contract, ((), ())), preferred_element_type...  74.6 us
    psum x1, blocking collectives, shards(): lax.psum(jnp.stack([attn_gain_grad, ffn_gain_grad]), ('ctx', 'fsdp'))  38.6 us
    ppermute x33, starting transfers between devices, swap(): return lax.ppermute(array, axis, [(i, i ^ bit) for i in range(size)])  38.3 us
    unnamed x304, local copies, waits for them, and re-layouts  25.5 us
    convert_element_type x42, other arithmetic, add(): return (one.astype(f32) + other.astype(f32)).astype(bf16)  23.8 us
    pallas_call x1, Pallas kernels, attention_backward(): pl.pallas_call(backward_kernel, out_shape=(jax.ShapeDtypeStruct((rows, wi...  21 us
  transfers between devices with their start and end apart: 93, of which 26 were waited for; matrix products, arithmetic and copies ran while one was open for 31% of the time, Pallas kernels for 2%

profile of v1, /device:TPU:0, one launch (start us, length us, event | category | flops | bytes accessed | tf_op | source)
XLA Modules:
  0.0 710.3 jit_solution(13841837188023226469)
XLA Ops:
  11.5 6.4 collective-permute-start.22
  22.5 6.5 all-gather
  52.0 5.5 collective-permute-done.23
  74.1 9.8 %collective-permute-done.5 = bf16[240,1280]{1,0:T(8,128)(2,1)} collective-permute-done((bf16[240,1280]{1,0:T(8,128)(2,1)}, bf16[240,1280]{1,0:T(8,128)(2,1)}, u32[]{:S(2)}, u32[]{:S(2)}) %collective-permute-start.5) | collective-permute-done | bytes 614432 | tf_op jit(solution)/shard_map/ppermute | solution.py:367
  87.9 8.5 %collective-permute-start.6 = (bf16[2,240,1280]{2,1,0:T(8,128)(2,1)}, bf16[2,240,1280]{2,1,0:T(8,128)(2,1)}, u32[]{:S(2)}, u32[]{:S(2)}) collective-permute-start(bf16[2,240,1280]{2,1,0:T(8,128)(2,1)} %pad_maximum_fusion.6), channel_id=1, source_target_pairs={{0,1},{1,0},{2,3},{3,2},{4,5},{5,4},{6,7},{7,6},{8,9},{9,8},{10,11... | collective-permute-start | bytes 3686408 | tf_op jit(solution)/shard_map/ppermute | solution.py:367
  99.0 7.0 concatenate.82
  107.6 7.7 %concatenate.79 = f32[512,960]{1,0:T(8,128)} concatenate(f32[512,32]{1,0:T(8,128)S(1)} %get-tuple-element.227, f32[512,32]{1,0:T(8,128)S(1)} %get-tuple-element.227, f32[512,32]{1,0:T(8,128)S(1)} %get-tuple-element.227, f32[512,32]{1,0:T(8,128)S(1)} %get-tuple-element.227, f32[512,32]{1,0:T(8,128)S(1)} %get-tuple-element.227, f32[512,32]{1,0:T(8,128)S(1)} %get-tuple-element.227, ...), dimensions={1} | concatenate | bytes 3932160 | tf_op jit(solution)/shard_map/concatenate | solution.py:241
  119.4 12.9 %collective-permute-done.14 = bf16[320,960]{1,0:T(8,128)(2,1)S(1)} collective-permute-done((bf16[320,960]{1,0:T(8,128)(2,1)}, bf16[320,960]{1,0:T(8,128)(2,1)S(1)}, u32[]{:S(2)}, u32[]{:S(2)}) %collective-permute-start.14) | collective-permute-done | bytes 614432 | tf_op jit(solution)/shard_map/ppermute | solution.py:367
  164.8 4.6 fusion.31
  179.8 5.3 fusion.93
  186.9 13.7 %attention_forward.1 = (bf16[512,960]{1,0:T(8,128)(2,1)S(1)}, f32[2,5,1,768]{3,2,1,0:T(1,128)S(1)}) custom-call(s32[1]{0:T(128)} %bitcast.12.member_ref, bf16[512,960]{1,0:T(8,128)(2,1)S(1)} %fusion.9.q_ref, bf16[1024,640]{1,0:T(8,128)(2,1)S(1)} %bitcast.636), custom_call_target="tpu_custom_call" | custom-call | flops 10066329600 | bytes 1966080 | tf_op jit(solution)/shard_map/attention_forward/pallas_call | solution.py:109
  213.7 9.0 %multiply_convert_fusion.1 = (bf16[512,2560]{1,0:T(8,128)(2,1)}, bf16[512,2560]{1,0:T(8,128)(2,1)}, bf16[512,2560]{1,0:T(8,128)(2,1)S(1)}) fusion(f32[512,2560]{1,0:T(8,128)} %fusion.93, f32[512,2560]{1,0:T(8,128)S(1)} %fusion.194, bf16[512,960]{0,1:T(8,128)(2,1)S(1)} %multiply_convert_fusion.3, bf16[960,2560]{1,0:T(8,128)(2,1)S(1)} %fusion.40), kind=kOutput, calls=%fused_computation.5 | convolution fusion | flops 2537553920 | bytes 24248320 | tf_op jit(solution)/shard_map/dot_general | solution.py:24
  238.9 4.6 convolution_convert_fusion
  244.9 21.0 %attention_backward.1 = (f32[512,960]{1,0:T(8,128)}, f32[1024,640]{1,0:T(8,128)}) custom-call(s32[1]{0:T(128)} %bitcast.12.member_ref, bf16[512,960]{1,0:T(8,128)(2,1)S(1)} %fusion.9.q_ref, bf16[1024,640]{1,0:T(8,128)(2,1)} %bitcast.637, bf16[512,960]{1,0:T(8,128)(2,1)S(1)} %get-tuple-element.15.mixed_ref, bf16[512,960]{1,0:T(8,128)(2,1)S(1)} %copy.255.grad_ref, ...), custom_call_target="tpu_custom_call" | custom-call | flops 25165824000 | bytes 5898240 | tf_op jit(solution)/shard_map/attention_backward/pallas_call | solution.py:199
  271.5 4.1 fusion.29
  278.1 4.5 convolution_convert_fusion.2
  282.6 4.4 convolution_convert_fusion.1
  299.9 11.1 %reshape.454 = bf16[2,2,640,960]{2,1,0,3:T(2,128)(2,1)} reshape(bf16[2560,960]{0,1:T(8,128)(2,1)} %convolution_convert_fusion) | data formatting | bytes 9830400 | tf_op jit(solution)/shard_map/reshape | solution.py:398
  311.0 4.1 select_bitcast_fusion.1
  315.1 4.2 select_bitcast_fusion.2
  319.4 6.9 fusion.178
  350.0 4.3 reshape.449
  357.8 4.2 fusion.22
  362.0 38.6 %psum.7 = f32[2,960]{1,0:T(2,128)S(1)} all-reduce(f32[2,960]{1,0:T(2,128)S(1)} %pad_maximum_fusion.30), channel_id=1, replica_groups=mesh['ctx'=8,'fsdp'=4] {'ctx','fsdp'}, use_global_device_ids=true, to_apply=%region_6.7 | all-reduce | flops 1920 | bytes 15360 | tf_op jit(solution)/shard_map/psum | solution.py:538
  406.7 3.9 collective-permute-start.27
  411.5 5.7 collective-permute-done.27
  419.0 7.1 collective-permute-done.28
  429.5 3.9 collective-permute-start.48
  445.4 11.2 %collective-permute-done.49 = bf16[240,320]{0,1:T(8,128)(2,1)S(1)} collective-permute-done((bf16[240,320]{0,1:T(8,128)(2,1)S(1)}, bf16[240,320]{0,1:T(8,128)(2,1)S(1)}, u32[]{:S(2)}, u32[]{:S(2)}) %collective-permute-start.49) | collective-permute-done | bytes 153632 | tf_op jit(solution)/shard_map/ppermute | solution.py:367
  461.3 3.9 collective-permute-start.51
  466.7 4.2 collective-permute-start.42
  472.3 4.3 collective-permute-start.52
  478.1 4.2 collective-permute-start.43
  487.0 14.2 %collective-permute-start.44 = (bf16[240,40]{0,1:T(8,128)(2,1)S(1)}, bf16[240,40]{0,1:T(8,128)(2,1)S(1)}, u32[]{:S(2)}, u32[]{:S(2)}) collective-permute-start(bf16[240,40]{0,1:T(8,128)(2,1)S(1)} %get-tuple-element.217), channel_id=1, source_target_pairs={{0,8},{4,12},{8,16},{12,20},{16,24},{20,28},{1,9},{5,13},{9,17},{1... | collective-permute-start | bytes 57608 | tf_op jit(solution)/shard_map/ppermute | solution.py:416
  503.2 3.7 collective-permute-done.47
  509.5 7.4 %collective-permute-done.31 = bf16[240,960]{1,0:T(8,128)(2,1)S(1)} collective-permute-done((bf16[240,960]{1,0:T(8,128)(2,1)S(1)}, bf16[240,960]{1,0:T(8,128)(2,1)S(1)}, u32[]{:S(2)}, u32[]{:S(2)}) %collective-permute-start.31) | collective-permute-done | bytes 460832 | tf_op jit(solution)/shard_map/ppermute | solution.py:367
  517.8 4.6 collective-permute-start.60
  524.7 4.6 collective-permute-start.33
  531.1 4.2 collective-permute-start.61
  537.2 4.3 collective-permute-start.34
  546.3 15.8 %collective-permute-start.35 = (bf16[240,120]{1,0:T(8,128)(2,1)S(1)}, bf16[240,120]{1,0:T(8,128)(2,1)S(1)}, u32[]{:S(2)}, u32[]{:S(2)}) collective-permute-start(bf16[240,120]{1,0:T(8,128)(2,1)S(1)} %get-tuple-element.193), channel_id=1, source_target_pairs={{0,8},{4,12},{8,16},{12,20},{16,24},{20,28},{1,9},{5,13},{9,17},{1... | collective-permute-start | bytes 172808 | tf_op jit(solution)/shard_map/ppermute | solution.py:416
  582.1 21.5 %collective-permute-done.67 = bf16[240,2560]{1,0:T(8,128)(2,1)S(1)} collective-permute-done((bf16[240,2560]{1,0:T(8,128)(2,1)}, bf16[240,2560]{1,0:T(8,128)(2,1)S(1)}, u32[]{:S(2)}, u32[]{:S(2)}) %collective-permute-start.67) | collective-permute-done | bytes 1228832 | tf_op jit(solution)/shard_map/ppermute | solution.py:367
  609.0 21.0 %collective-permute-done.76 = bf16[240,2560]{1,0:T(8,128)(2,1)} collective-permute-done((bf16[240,2560]{1,0:T(8,128)(2,1)}, bf16[240,2560]{1,0:T(8,128)(2,1)}, u32[]{:S(2)}, u32[]{:S(2)}) %collective-permute-start.76) | collective-permute-done | bytes 1228832 | tf_op jit(solution)/shard_map/ppermute | solution.py:367
  636.1 7.1 %collective-permute-done.85 = bf16[640,960]{0,1:T(8,128)(2,1)} collective-permute-done((bf16[640,960]{0,1:T(8,128)(2,1)}, bf16[640,960]{0,1:T(8,128)(2,1)}, u32[]{:S(2)}, u32[]{:S(2)}) %collective-permute-start.85) | collective-permute-done | bytes 1228832 | tf_op jit(solution)/shard_map/ppermute | solution.py:367
  651.7 5.2 collective-permute-start.69
  685.5 5.2 collective-permute-start.89
  696.1 4.1 collective-permute-done.74
  701.1 4.7 collective-permute-done.83
  (686 shorter events, 321.5 us)
Async XLA Ops:
  4.4 64.6 %collective-permute-start.3 = (bf16[2,64,962]{2,1,0:T(8,128)(2,1)}, bf16[2,64,962]{2,1,0:T(8,128)(2,1)S(1)}, u32[]{:S(2)}, u32[]{:S(2)}) collective-permute-start(bf16[2,64,962]{2,1,0:T(8,128)(2,1)} %get-tuple-element.133), channel_id=1, source_target_pairs={{0,0},{1,16},{2,2},{3,18},{4,4},{5,20},{6,6},{7,22},{8,8},{9,24},{... | collective-permute-start | bytes 738824 | tf_op jit(solution)/shard_map/ppermute | solution.py:306
  6.0 62.9 %collective-permute-start.2 = (bf16[2,64,962]{2,1,0:T(8,128)(2,1)}, bf16[2,64,962]{2,1,0:T(8,128)(2,1)S(1)}, u32[]{:S(2)}, u32[]{:S(2)}) collective-permute-start(bf16[2,64,962]{2,1,0:T(8,128)(2,1)} %get-tuple-element.134), channel_id=1, source_target_pairs={{0,4},{1,20},{2,6},{3,22},{4,8},{5,24},{6,10},{7,26},{8,12},{9,28}... | collective-permute-start | bytes 738824 | tf_op jit(solution)/shard_map/ppermute | solution.py:306
  8.9 57.4 %collective-permute-start.1 = (bf16[2,64,962]{2,1,0:T(8,128)(2,1)}, bf16[2,64,962]{2,1,0:T(8,128)(2,1)}, u32[]{:S(2)}, u32[]{:S(2)}) collective-permute-start(bf16[2,64,962]{2,1,0:T(8,128)(2,1)} %get-tuple-element.135), channel_id=1, source_target_pairs={{0,8},{1,24},{2,10},{3,26},{4,12},{5,28},{6,14},{7,30},{8,0},{9,16... | collective-permute-start | bytes 738824 | tf_op jit(solution)/shard_map/ppermute | solution.py:306
  11.5 38.8 %collective-permute-start.22 = (bf16[2,64,960]{2,1,0:T(8,128)(2,1)}, bf16[2,64,960]{2,1,0:T(8,128)(2,1)}, u32[]{:S(2)}, u32[]{:S(2)}) collective-permute-start(bf16[2,64,960]{2,1,0:T(8,128)(2,1)} %get-tuple-element.126), channel_id=1, source_target_pairs={{0,8},{1,24},{2,10},{3,26},{4,12},{5,28},{6,14},{7,30},{8,0},{9,16... | collective-permute-start | bytes 737288 | tf_op jit(solution)/shard_map/ppermute | solution.py:306
  17.9 29.5 %collective-permute-start.21 = (bf16[2,64,960]{2,1,0:T(8,128)(2,1)}, bf16[2,64,960]{2,1,0:T(8,128)(2,1)}, u32[]{:S(2)}, u32[]{:S(2)}) collective-permute-start(bf16[2,64,960]{2,1,0:T(8,128)(2,1)} %get-tuple-element.127), channel_id=1, source_target_pairs={{0,12},{1,28},{2,14},{3,30},{4,0},{5,16},{6,2},{7,18},{8,4},{9,20}... | collective-permute-start | bytes 737288 | tf_op jit(solution)/shard_map/ppermute | solution.py:306
  65.8 49.6 %collective-permute-start.13 = (bf16[320,960]{1,0:T(8,128)(2,1)}, bf16[320,960]{1,0:T(8,128)(2,1)}, u32[]{:S(2)}, u32[]{:S(2)}) collective-permute-start(bf16[320,960]{1,0:T(8,128)(2,1)} %get-tuple-element.166), channel_id=1, source_target_pairs={{0,2},{1,3},{2,0},{3,1},{4,6},{5,7},{6,4},{7,5},{8,10},{9,11},{10,... | collective-permute-start | bytes 1843208 | tf_op jit(solution)/shard_map/ppermute | solution.py:367
  66.4 71.4 %collective-permute-start.9 = (bf16[240,2560]{1,0:T(8,128)(2,1)}, bf16[240,2560]{1,0:T(8,128)(2,1)}, u32[]{:S(2)}, u32[]{:S(2)}) collective-permute-start(bf16[240,2560]{1,0:T(8,128)(2,1)} %get-tuple-element.116), channel_id=1, source_target_pairs={{0,2},{1,3},{2,0},{3,1},{4,6},{5,7},{6,4},{7,5},{8,10},{9,11},{10,... | collective-permute-start | bytes 3686408 | tf_op jit(solution)/shard_map/ppermute | solution.py:367
  87.9 51.6 %collective-permute-start.6 = (bf16[2,240,1280]{2,1,0:T(8,128)(2,1)}, bf16[2,240,1280]{2,1,0:T(8,128)(2,1)}, u32[]{:S(2)}, u32[]{:S(2)}) collective-permute-start(bf16[2,240,1280]{2,1,0:T(8,128)(2,1)} %pad_maximum_fusion.6), channel_id=1, source_target_pairs={{0,1},{1,0},{2,3},{3,2},{4,5},{5,4},{6,7},{7,6},{8,9},{9,8},{10,11... | collective-permute-start | bytes 3686408 | tf_op jit(solution)/shard_map/ppermute | solution.py:367
  115.4 16.9 %collective-permute-start.14 = (bf16[320,960]{1,0:T(8,128)(2,1)}, bf16[320,960]{1,0:T(8,128)(2,1)S(1)}, u32[]{:S(2)}, u32[]{:S(2)}) collective-permute-start(bf16[320,960]{1,0:T(8,128)(2,1)} %collective-permute-done.13), channel_id=1, source_target_pairs={{0,4},{4,0},{8,12},{12,8},{16,20},{20,16},{24,28},{28,24},{1,5},{5... | collective-permute-start | bytes 1843208 | tf_op jit(solution)/shard_map/ppermute | solution.py:367
  119.3 24.1 %collective-permute-start.7 = (bf16[2,240,1280]{2,1,0:T(8,128)(2,1)S(1)}, bf16[2,240,1280]{2,1,0:T(8,128)(2,1)S(1)}, u32[]{:S(2)}, u32[]{:S(2)}) collective-permute-start(bf16[2,240,1280]{2,1,0:T(8,128)(2,1)S(1)} %pad_maximum_fusion.7), channel_id=1, source_target_pairs={{0,1},{1,0},{2,3},{3,2},{4,5},{5,4},{6,7},{7,6},{8,9},{9,8},{10,11... | collective-permute-start | bytes 3686408 | tf_op jit(solution)/shard_map/ppermute | solution.py:367
  136.1 16.6 %collective-permute-start.16 = (bf16[2,320,960]{2,1,0:T(8,128)(2,1)}, bf16[2,320,960]{2,1,0:T(8,128)(2,1)}, u32[]{:S(2)}, u32[]{:S(2)}) collective-permute-start(bf16[2,320,960]{2,1,0:T(8,128)(2,1)} %pad_maximum_fusion.5), channel_id=1, source_target_pairs={{0,1},{1,0},{2,3},{3,2},{4,5},{5,4},{6,7},{7,6},{8,9},{9,8},{10,11... | collective-permute-start | bytes 3686408 | tf_op jit(solution)/shard_map/ppermute | solution.py:367
  137.3 19.3 %collective-permute-start.15 = (bf16[2,320,960]{2,1,0:T(8,128)(2,1)}, bf16[2,320,960]{2,1,0:T(8,128)(2,1)}, u32[]{:S(2)}, u32[]{:S(2)}) collective-permute-start(bf16[2,320,960]{2,1,0:T(8,128)(2,1)} %pad_maximum_fusion.4), channel_id=1, source_target_pairs={{0,1},{1,0},{2,3},{3,2},{4,5},{5,4},{6,7},{7,6},{8,9},{9,8},{10,11... | collective-permute-start | bytes 3686408 | tf_op jit(solution)/shard_map/ppermute | solution.py:367
  137.8 32.6 %collective-permute-start.10 = (bf16[240,2560]{1,0:T(8,128)(2,1)}, bf16[240,2560]{1,0:T(8,128)(2,1)}, u32[]{:S(2)}, u32[]{:S(2)}) collective-permute-start(bf16[240,2560]{1,0:T(8,128)(2,1)} %collective-permute-done.9), channel_id=1, source_target_pairs={{0,4},{4,0},{8,12},{12,8},{16,20},{20,16},{24,28},{28,24},{1,5},{5... | collective-permute-start | bytes 3686408 | tf_op jit(solution)/shard_map/ppermute | solution.py:367
  152.6 32.5 %collective-permute-start.8 = (bf16[512,640]{1,0:T(8,128)(2,1)}, bf16[512,640]{1,0:T(8,128)(2,1)}, u32[]{:S(2)}, u32[]{:S(2)}) collective-permute-start(bf16[512,640]{1,0:T(8,128)(2,1)} %pad_maximum_fusion.14), channel_id=1, source_target_pairs={{0,1},{1,0},{2,3},{3,2},{4,5},{5,4},{6,7},{7,6},{8,9},{9,8},{10,11... | collective-permute-start | bytes 1966088 | tf_op jit(solution)/shard_map/ppermute | solution.py:335
  175.5 28.9 %collective-permute-start.12 = (bf16[2,240,2560]{2,1,0:T(8,128)(2,1)}, bf16[2,240,2560]{2,1,0:T(8,128)(2,1)}, u32[]{:S(2)}, u32[]{:S(2)}) collective-permute-start(bf16[2,240,2560]{2,1,0:T(8,128)(2,1)} %pad_maximum_fusion.2), channel_id=1, source_target_pairs={{0,1},{1,0},{2,3},{3,2},{4,5},{5,4},{6,7},{7,6},{8,9},{9,8},{10,11... | collective-permute-start | bytes 7372808 | tf_op jit(solution)/shard_map/ppermute | solution.py:367
  177.6 33.2 %collective-permute-start.11 = (bf16[2,240,2560]{2,1,0:T(8,128)(2,1)}, bf16[2,240,2560]{2,1,0:T(8,128)(2,1)}, u32[]{:S(2)}, u32[]{:S(2)}) collective-permute-start(bf16[2,240,2560]{2,1,0:T(8,128)(2,1)} %pad_maximum_fusion.1), channel_id=1, source_target_pairs={{0,1},{1,0},{2,3},{3,2},{4,5},{5,4},{6,7},{7,6},{8,9},{9,8},{10,11... | collective-permute-start | bytes 7372808 | tf_op jit(solution)/shard_map/ppermute | solution.py:367
  288.4 45.5 %collective-permute-start.20 = (bf16[2,64,960]{2,1,0:T(8,128)(2,1)S(1)}, bf16[2,64,960]{2,1,0:T(8,128)(2,1)S(1)}, u32[]{:S(2)}, u32[]{:S(2)}) collective-permute-start(bf16[2,64,960]{2,1,0:T(8,128)(2,1)S(1)} %get-tuple-element.129), channel_id=1, source_target_pairs={{12,0},{28,1},{14,2},{30,3},{0,4},{16,5},{2,6},{18,7},{4,8},{20,9}... | collective-permute-start | bytes 737288 | tf_op jit(solution)/shard_map/ppermute | solution.py:327
  288.6 44.5 %collective-permute-start.17 = (bf16[2,64,960]{2,1,0:T(8,128)(2,1)}, bf16[2,64,960]{2,1,0:T(8,128)(2,1)S(1)}, u32[]{:S(2)}, u32[]{:S(2)}) collective-permute-start(bf16[2,64,960]{2,1,0:T(8,128)(2,1)} %get-tuple-element.130), channel_id=1, source_target_pairs={{0,0},{16,1},{2,2},{18,3},{4,4},{20,5},{6,6},{22,7},{8,8},{24,9},{... | collective-permute-start | bytes 737288 | tf_op jit(solution)/shard_map/ppermute | solution.py:327
  290.2 43.0 %collective-permute-start.18 = (bf16[2,64,960]{2,1,0:T(8,128)(2,1)S(1)}, bf16[2,64,960]{2,1,0:T(8,128)(2,1)S(1)}, u32[]{:S(2)}, u32[]{:S(2)}) collective-permute-start(bf16[2,64,960]{2,1,0:T(8,128)(2,1)S(1)} %get-tuple-element.131), channel_id=1, source_target_pairs={{4,0},{20,1},{6,2},{22,3},{8,4},{24,5},{10,6},{26,7},{12,8},{28,9}... | collective-permute-start | bytes 737288 | tf_op jit(solution)/shard_map/ppermute | solution.py:327
  292.9 40.9 %collective-permute-start.19 = (bf16[2,64,960]{2,1,0:T(8,128)(2,1)S(1)}, bf16[2,64,960]{2,1,0:T(8,128)(2,1)S(1)}, u32[]{:S(2)}, u32[]{:S(2)}) collective-permute-start(bf16[2,64,960]{2,1,0:T(8,128)(2,1)S(1)} %get-tuple-element.132), channel_id=1, source_target_pairs={{8,0},{24,1},{10,2},{26,3},{12,4},{28,5},{14,6},{30,7},{0,8},{16,9... | collective-permute-start | bytes 737288 | tf_op jit(solution)/shard_map/ppermute | solution.py:327
  295.6 39.5 %collective-permute-start.25 = (bf16[512,640]{1,0:T(8,128)(2,1)S(1)}, bf16[512,640]{1,0:T(8,128)(2,1)}, u32[]{:S(2)}, u32[]{:S(2)}) collective-permute-start(bf16[512,640]{1,0:T(8,128)(2,1)S(1)} %pad_maximum_fusion.15), channel_id=1, source_target_pairs={{0,1},{1,0},{2,3},{3,2},{4,5},{5,4},{6,7},{7,6},{8,9},{9,8},{10,11... | collective-permute-start | bytes 1966088 | tf_op jit(solution)/shard_map/ppermute | solution.py:361
  333.1 102.1 %collective-permute-start.57 = (bf16[2,240,960]{2,1,0:T(8,128)(2,1)}, bf16[2,240,960]{2,1,0:T(8,128)(2,1)}, u32[]{:S(2)}, u32[]{:S(2)}) collective-permute-start(bf16[2,240,960]{2,1,0:T(8,128)(2,1)} %select_bitcast_fusion.6), channel_id=1, source_target_pairs={{0,1},{1,0},{2,3},{3,2},{4,5},{5,4},{6,7},{7,6},{8,9},{9,8},{10,11... | collective-permute-start | bytes 2764808 | tf_op jit(solution)/shard_map/ppermute | solution.py:367
  333.2 104.4 %collective-permute-start.30 = (bf16[2,240,960]{2,1,0:T(8,128)(2,1)}, bf16[2,240,960]{2,1,0:T(8,128)(2,1)}, u32[]{:S(2)}, u32[]{:S(2)}) collective-permute-start(bf16[2,240,960]{2,1,0:T(8,128)(2,1)} %select_bitcast_fusion.7), channel_id=1, source_target_pairs={{0,1},{1,0},{2,3},{3,2},{4,5},{5,4},{6,7},{7,6},{8,9},{9,8},{10,11... | collective-permute-start | bytes 2764808 | tf_op jit(solution)/shard_map/ppermute | solution.py:367
  333.8 235.4 %collective-permute-start.66 = (bf16[2,240,2560]{2,1,0:T(8,128)(2,1)}, bf16[2,240,2560]{2,1,0:T(8,128)(2,1)}, u32[]{:S(2)}, u32[]{:S(2)}) collective-permute-start(bf16[2,240,2560]{2,1,0:T(8,128)(2,1)} %select_bitcast_fusion.2), channel_id=1, source_target_pairs={{0,1},{1,0},{2,3},{3,2},{4,5},{5,4},{6,7},{7,6},{8,9},{9,8},{10,11... | collective-permute-start | bytes 7372808 | tf_op jit(solution)/shard_map/ppermute | solution.py:367
  411.4 14.6 %collective-permute-start.28 = (bf16[2,64,960]{2,1,0:T(8,128)(2,1)S(1)}, bf16[2,64,960]{2,1,0:T(8,128)(2,1)S(1)}, u32[]{:S(2)}, u32[]{:S(2)}) collective-permute-start(bf16[2,64,960]{2,1,0:T(8,128)(2,1)S(1)} %get-tuple-element.124), channel_id=1, source_target_pairs={{8,0},{24,1},{10,2},{26,3},{12,4},{28,5},{14,6},{30,7},{0,8},{16,9... | collective-permute-start | bytes 737288 | tf_op jit(solution)/shard_map/ppermute | solution.py:327
  426.1 147.7 %collective-permute-start.75 = (bf16[2,240,2560]{2,1,0:T(8,128)(2,1)}, bf16[2,240,2560]{2,1,0:T(8,128)(2,1)S(1)}, u32[]{:S(2)}, u32[]{:S(2)}) collective-permute-start(bf16[2,240,2560]{2,1,0:T(8,128)(2,1)} %select_bitcast_fusion.1), channel_id=1, source_target_pairs={{0,1},{1,0},{2,3},{3,2},{4,5},{5,4},{6,7},{7,6},{8,9},{9,8},{10,11... | collective-permute-start | bytes 7372808 | tf_op jit(solution)/shard_map/ppermute | solution.py:367
  437.6 70.0 %collective-permute-start.58 = (bf16[240,960]{1,0:T(8,128)(2,1)S(1)}, bf16[240,960]{1,0:T(8,128)(2,1)S(1)}, u32[]{:S(2)}, u32[]{:S(2)}) collective-permute-start(bf16[240,960]{1,0:T(8,128)(2,1)S(1)} %select_bitcast_fusion.8), channel_id=1, source_target_pairs={{0,2},{1,3},{2,0},{3,1},{4,6},{5,7},{6,4},{7,5},{8,10},{9,11},{10,... | collective-permute-start | bytes 1382408 | tf_op jit(solution)/shard_map/ppermute | solution.py:367
  443.1 13.5 %collective-permute-start.49 = (bf16[240,320]{0,1:T(8,128)(2,1)S(1)}, bf16[240,320]{0,1:T(8,128)(2,1)S(1)}, u32[]{:S(2)}, u32[]{:S(2)}) collective-permute-start(bf16[240,320]{0,1:T(8,128)(2,1)S(1)} %select_bitcast_fusion.12), channel_id=1, source_target_pairs={{0,2},{1,3},{2,0},{3,1},{4,6},{5,7},{6,4},{7,5},{8,10},{9,11},{10,... | collective-permute-start | bytes 460808 | tf_op jit(solution)/shard_map/ppermute | solution.py:367
  443.3 16.1 %collective-permute-start.40 = (bf16[240,320]{0,1:T(8,128)(2,1)S(1)}, bf16[240,320]{0,1:T(8,128)(2,1)S(1)}, u32[]{:S(2)}, u32[]{:S(2)}) collective-permute-start(bf16[240,320]{0,1:T(8,128)(2,1)S(1)} %select_bitcast_fusion.13), channel_id=1, source_target_pairs={{0,2},{1,3},{2,0},{3,1},{4,6},{5,7},{6,4},{7,5},{8,10},{9,11},{10,... | collective-permute-start | bytes 460808 | tf_op jit(solution)/shard_map/ppermute | solution.py:367
  485.7 15.6 %collective-permute-start.56 = (bf16[240,40]{0,1:T(8,128)(2,1)S(1)}, bf16[240,40]{0,1:T(8,128)(2,1)S(1)}, u32[]{:S(2)}, u32[]{:S(2)}) collective-permute-start(bf16[240,40]{0,1:T(8,128)(2,1)S(1)} %fusion.133), channel_id=1, source_target_pairs={{24,16},{28,20},{16,8},{20,12},{8,0},{12,4},{25,17},{29,21},{17,9}... | collective-permute-start | bytes 57608 | tf_op jit(solution)/shard_map/ppermute | solution.py:416
  487.0 16.2 %collective-permute-start.44 = (bf16[240,40]{0,1:T(8,128)(2,1)S(1)}, bf16[240,40]{0,1:T(8,128)(2,1)S(1)}, u32[]{:S(2)}, u32[]{:S(2)}) collective-permute-start(bf16[240,40]{0,1:T(8,128)(2,1)S(1)} %get-tuple-element.217), channel_id=1, source_target_pairs={{0,8},{4,12},{8,16},{12,20},{16,24},{20,28},{1,9},{5,13},{9,17},{1... | collective-permute-start | bytes 57608 | tf_op jit(solution)/shard_map/ppermute | solution.py:416
  503.2 74.3 %collective-permute-start.84 = (bf16[2,640,960]{1,2,0:T(8,128)(2,1)}, bf16[2,640,960]{1,2,0:T(8,128)(2,1)}, u32[]{:S(2)}, u32[]{:S(2)}) collective-permute-start(bf16[2,640,960]{1,2,0:T(8,128)(2,1)} %select_bitcast_fusion), channel_id=1, source_target_pairs={{0,1},{1,0},{2,3},{3,2},{4,5},{5,4},{6,7},{7,6},{8,9},{9,8},{10,11... | collective-permute-start | bytes 7372808 | tf_op jit(solution)/shard_map/ppermute | solution.py:367
  545.0 17.4 %collective-permute-start.65 = (bf16[240,120]{1,0:T(8,128)(2,1)S(1)}, bf16[240,120]{1,0:T(8,128)(2,1)S(1)}, u32[]{:S(2)}, u32[]{:S(2)}) collective-permute-start(bf16[240,120]{1,0:T(8,128)(2,1)S(1)} %fusion.119), channel_id=1, source_target_pairs={{24,16},{28,20},{16,8},{20,12},{8,0},{12,4},{25,17},{29,21},{17,9}... | collective-permute-start | bytes 172808 | tf_op jit(solution)/shard_map/ppermute | solution.py:416
  546.3 18.4 %collective-permute-start.35 = (bf16[240,120]{1,0:T(8,128)(2,1)S(1)}, bf16[240,120]{1,0:T(8,128)(2,1)S(1)}, u32[]{:S(2)}, u32[]{:S(2)}) collective-permute-start(bf16[240,120]{1,0:T(8,128)(2,1)S(1)} %get-tuple-element.193), channel_id=1, source_target_pairs={{0,8},{4,12},{8,16},{12,20},{16,24},{20,28},{1,9},{5,13},{9,17},{1... | collective-permute-start | bytes 172808 | tf_op jit(solution)/shard_map/ppermute | solution.py:416
  573.4 30.2 %collective-permute-start.67 = (bf16[240,2560]{1,0:T(8,128)(2,1)}, bf16[240,2560]{1,0:T(8,128)(2,1)S(1)}, u32[]{:S(2)}, u32[]{:S(2)}) collective-permute-start(bf16[240,2560]{1,0:T(8,128)(2,1)} %select_bitcast_fusion.5), channel_id=1, source_target_pairs={{0,2},{1,3},{2,0},{3,1},{4,6},{5,7},{6,4},{7,5},{8,10},{9,11},{10,... | collective-permute-start | bytes 3686408 | tf_op jit(solution)/shard_map/ppermute | solution.py:367
  575.9 54.1 %collective-permute-start.76 = (bf16[240,2560]{1,0:T(8,128)(2,1)}, bf16[240,2560]{1,0:T(8,128)(2,1)}, u32[]{:S(2)}, u32[]{:S(2)}) collective-permute-start(bf16[240,2560]{1,0:T(8,128)(2,1)} %select_bitcast_fusion.4), channel_id=1, source_target_pairs={{0,2},{1,3},{2,0},{3,1},{4,6},{5,7},{6,4},{7,5},{8,10},{9,11},{10,... | collective-permute-start | bytes 3686408 | tf_op jit(solution)/shard_map/ppermute | solution.py:367
  581.7 61.5 %collective-permute-start.85 = (bf16[640,960]{0,1:T(8,128)(2,1)}, bf16[640,960]{0,1:T(8,128)(2,1)}, u32[]{:S(2)}, u32[]{:S(2)}) collective-permute-start(bf16[640,960]{0,1:T(8,128)(2,1)} %select_bitcast_fusion.3), channel_id=1, source_target_pairs={{0,2},{1,3},{2,0},{3,1},{4,6},{5,7},{6,4},{7,5},{8,10},{9,11},{10,... | collective-permute-start | bytes 3686408 | tf_op jit(solution)/shard_map/ppermute | solution.py:367
  607.0 40.6 %collective-permute-start.68 = (bf16[4,240,320]{1,2,0:T(8,128)(2,1)}, bf16[4,240,320]{1,2,0:T(8,128)(2,1)}, u32[]{:S(2)}, u32[]{:S(2)}) collective-permute-start(bf16[4,240,320]{1,2,0:T(8,128)(2,1)} %copy.268), channel_id=1, source_target_pairs={{0,4},{4,0},{8,12},{12,8},{16,20},{20,16},{24,28},{28,24},{1,5},{5... | collective-permute-start | bytes 1843208 | tf_op jit(solution)/shard_map/ppermute | solution.py:367
  634.7 23.6 %collective-permute-start.77 = (bf16[4,240,320]{1,2,0:T(8,128)(2,1)}, bf16[4,240,320]{1,2,0:T(8,128)(2,1)}, u32[]{:S(2)}, u32[]{:S(2)}) collective-permute-start(bf16[4,240,320]{1,2,0:T(8,128)(2,1)} %copy.272), channel_id=1, source_target_pairs={{0,4},{4,0},{8,12},{12,8},{16,20},{20,16},{24,28},{28,24},{1,5},{5... | collective-permute-start | bytes 1843208 | tf_op jit(solution)/shard_map/ppermute | solution.py:367
  646.2 17.3 %collective-permute-start.86 = (bf16[4,640,120]{1,2,0:T(8,128)(2,1)}, bf16[4,640,120]{1,2,0:T(8,128)(2,1)}, u32[]{:S(2)}, u32[]{:S(2)}) collective-permute-start(bf16[4,640,120]{1,2,0:T(8,128)(2,1)} %broadcast_select_fusion.10), channel_id=1, source_target_pairs={{0,4},{4,0},{8,12},{12,8},{16,20},{20,16},{24,28},{28,24},{1,5},{5... | collective-permute-start | bytes 1843208 | tf_op jit(solution)/shard_map/ppermute | solution.py:367
  651.7 14.6 %collective-permute-start.69 = (bf16[240,320]{1,0:T(8,128)(2,1)}, bf16[240,320]{1,0:T(8,128)(2,1)}, u32[]{:S(2)}, u32[]{:S(2)}) collective-permute-start(bf16[240,320]{1,0:T(8,128)(2,1)} %get-tuple-element.155), channel_id=1, source_target_pairs={{0,8},{4,12},{1,9},{5,13},{2,10},{6,14},{3,11},{7,15}} | collective-permute-start | bytes 460808 | tf_op jit(solution)/shard_map/ppermute | solution.py:416
  656.9 18.2 %collective-permute-start.72 = (bf16[240,320]{1,0:T(8,128)(2,1)}, bf16[240,320]{1,0:T(8,128)(2,1)}, u32[]{:S(2)}, u32[]{:S(2)}) collective-permute-start(bf16[240,320]{1,0:T(8,128)(2,1)} %get-tuple-element.156), channel_id=1, source_target_pairs={{24,16},{28,20},{25,17},{29,21},{26,18},{30,22},{27,19},{31,23}} | collective-permute-start | bytes 460808 | tf_op jit(solution)/shard_map/ppermute | solution.py:416
  662.8 18.5 %collective-permute-start.81 = (bf16[240,320]{1,0:T(8,128)(2,1)S(1)}, bf16[240,320]{1,0:T(8,128)(2,1)S(1)}, u32[]{:S(2)}, u32[]{:S(2)}) collective-permute-start(bf16[240,320]{1,0:T(8,128)(2,1)S(1)} %get-tuple-element.152), channel_id=1, source_target_pairs={{24,16},{28,20},{25,17},{29,21},{26,18},{30,22},{27,19},{31,23}} | collective-permute-start | bytes 460808 | tf_op jit(solution)/shard_map/ppermute | solution.py:416
  666.3 18.4 %collective-permute-start.90 = (bf16[640,120]{0,1:T(8,128)(2,1)S(1)}, bf16[640,120]{0,1:T(8,128)(2,1)S(1)}, u32[]{:S(2)}, u32[]{:S(2)}) collective-permute-start(bf16[640,120]{0,1:T(8,128)(2,1)S(1)} %get-tuple-element.172), channel_id=1, source_target_pairs={{24,16},{28,20},{25,17},{29,21},{26,18},{30,22},{27,19},{31,23}} | collective-permute-start | bytes 460808 | tf_op jit(solution)/shard_map/ppermute | solution.py:416
  678.1 16.7 %collective-permute-start.71 = (bf16[240,320]{1,0:T(8,128)(2,1)S(1)}, bf16[240,320]{1,0:T(8,128)(2,1)S(1)}, u32[]{:S(2)}, u32[]{:S(2)}) collective-permute-start(bf16[240,320]{1,0:T(8,128)(2,1)S(1)} %get-tuple-element.153), channel_id=1, source_target_pairs={{0,8},{4,12},{8,16},{12,20},{16,24},{20,28},{1,9},{5,13},{9,17},{1... | collective-permute-start | bytes 460808 | tf_op jit(solution)/shard_map/ppermute | solution.py:416
  682.2 19.0 %collective-permute-start.80 = (bf16[240,320]{1,0:T(8,128)(2,1)S(1)}, bf16[240,320]{1,0:T(8,128)(2,1)S(1)}, u32[]{:S(2)}, u32[]{:S(2)}) collective-permute-start(bf16[240,320]{1,0:T(8,128)(2,1)S(1)} %get-tuple-element.149), channel_id=1, source_target_pairs={{0,8},{4,12},{8,16},{12,20},{16,24},{20,28},{1,9},{5,13},{9,17},{1... | collective-permute-start | bytes 460808 | tf_op jit(solution)/shard_map/ppermute | solution.py:416
  685.5 21.3 %collective-permute-start.89 = (bf16[640,120]{0,1:T(8,128)(2,1)S(1)}, bf16[640,120]{0,1:T(8,128)(2,1)S(1)}, u32[]{:S(2)}, u32[]{:S(2)}) collective-permute-start(bf16[640,120]{0,1:T(8,128)(2,1)S(1)} %get-tuple-element.169), channel_id=1, source_target_pairs={{0,8},{4,12},{8,16},{12,20},{16,24},{20,28},{1,9},{5,13},{9,17},{1... | collective-permute-start | bytes 460808 | tf_op jit(solution)/shard_map/ppermute | solution.py:416
  694.8 13.6 %collective-permute-start.92 = (bf16[640,120]{0,1:T(8,128)(2,1)}, bf16[640,120]{0,1:T(8,128)(2,1)}, u32[]{:S(2)}, u32[]{:S(2)}) collective-permute-start(bf16[640,120]{0,1:T(8,128)(2,1)} %fusion.89), channel_id=1, source_target_pairs={{24,16},{28,20},{16,8},{20,12},{8,0},{12,4},{25,17},{29,21},{17,9}... | collective-permute-start | bytes 460808 | tf_op jit(solution)/shard_map/ppermute | solution.py:416
  (180 other events, 1319.4 us)
